TPU v7x, 256 devices: a whole 4x4x8 slice. The times are simulated.
256 devices in a mesh: dp: 16 (over x, y), seq: 16 (over z, core).
Axes of the slice: x: 4, y: 4, z: 8, core: 2. Of those that a mesh axis runs over, the one named last changes fastest.
Arguments:
- queries: bfloat16 [16, 2048, 2048], P('dp', 'seq'), may hold values from -6 to 6
- attended_grad: bfloat16 [16, 2048, 2048], P('dp', 'seq'), may hold values from -6 to 6
- neighbour_pool: bfloat16 [16, 64, 128, 896], P('dp', 'seq'), may hold values from -6 to 6
- stretch_slot: int32 [16, 32], P('dp'), may hold values from 0 to 63, as said below
- enc_gain: float32 [896], replicated, may hold values from 0.1 to 1.9
- enc_up: bfloat16 [896, 1792], replicated, may hold values from -0.1875 to 0.1875
- enc_down: bfloat16 [1792, 896], replicated, may hold values from -0.125 to 0.125
- key_weight: bfloat16 [896, 2048], P(None, 'seq'), may hold values from -0.1875 to 0.1875
- value_weight: bfloat16 [896, 2048], P(None, 'seq'), may hold values from -0.1875 to 0.1875
Outputs:
- attended: bfloat16 [16, 2048, 2048], P('dp', 'seq')
- query_grad: bfloat16 [16, 2048, 2048], P('dp', 'seq')
- pool_grad: bfloat16 [16, 64, 128, 896], P('dp', 'seq')
- key_weight_grad: float32 [896, 2048], P(None, 'seq')
- value_weight_grad: float32 [896, 2048], P(None, 'seq')
Inputs may be any that keep to these rules, and one draw needn't show every extreme that they name: `stretch_slot`: slot s is held by the device s // 4 along seq. No slot is named twice within a sequence, and in every sequence some device holds 4 named slots.
All inputs are finite; a program needn't handle non-finite values.
Results may differ from a plain program's by a relative error of at most 0.03.
Values may be sent and summed in bfloat16 or wider, within the bound.
A program may use at most 128 MiB of HBM per device.

v0:
```python
import math

import jax
import jax.numpy as jnp
from jax import lax
from jax.sharding import PartitionSpec as P

STRETCH = 64
HD = 128


epsilon = 1e-06


def encode_rows(row_block, gain_vector, up_matrix, down_matrix):
    row_values = row_block.astype(jnp.float32)
    inverse = lax.rsqrt(jnp.mean(row_values * row_values, axis=-1, keepdims=True) + epsilon)
    normed = (row_values * inverse * gain_vector).astype(jnp.bfloat16)
    before = jnp.dot(normed, up_matrix, preferred_element_type=jnp.float32)
    activity = jax.nn.gelu(before).astype(jnp.bfloat16)
    encoded = (
        row_values + jnp.dot(activity, down_matrix, preferred_element_type=jnp.float32)
    ).astype(jnp.bfloat16)
    return (encoded, before, inverse)


def encode_backward(encoded_grad, row_block, before, inverse, gain_vector, up_matrix, down_matrix):
    activity_grad = jnp.einsum(
        "rd,fd->rf", encoded_grad, down_matrix, preferred_element_type=jnp.float32
    )
    unused_value, gelu_back = jax.vjp(jax.nn.gelu, before)
    before_grad = gelu_back(activity_grad)[0].astype(jnp.bfloat16)
    normed_grad = jnp.einsum(
        "rf,df->rd", before_grad, up_matrix, preferred_element_type=jnp.float32
    )
    row_values = row_block.astype(jnp.float32)
    scaled_grad = gain_vector * normed_grad
    cubed = inverse * inverse * inverse
    result = (
        encoded_grad.astype(jnp.float32)
        + inverse * scaled_grad
        - row_values * cubed * jnp.mean(row_values * scaled_grad, axis=-1, keepdims=True)
    )
    return result.astype(jnp.bfloat16)


def on_device(
    queries,
    attended_grad,
    neighbour_pool,
    stretch_slot,
    enc_gain,
    enc_up,
    enc_down,
    key_weight,
    value_weight,
):
    groups = lax.axis_size("seq")
    token_count = queries.shape[1]
    stretch_count = token_count // STRETCH
    holding = neighbour_pool.shape[1]
    neighbour_span = neighbour_pool.shape[2]
    feature_width = neighbour_pool.shape[3]
    piece_rows = neighbour_span // groups
    all_slots = stretch_slot[0]
    total_stretches = all_slots.shape[0]
    middle_index = all_slots % holding * groups + all_slots // holding
    flat_position = jnp.arange(holding * groups, dtype=jnp.int32)
    position_slot = flat_position % groups * holding + flat_position // groups
    slot_match = all_slots[:, None] == position_slot[None, :]
    slot_user = jnp.sum(
        jnp.where(slot_match, jnp.arange(total_stretches, dtype=jnp.int32)[:, None], 0), axis=0
    )
    slot_named = jnp.any(slot_match, axis=0)
    pool_rows = neighbour_pool[0]
    pool_flat = pool_rows.reshape(holding * neighbour_span, feature_width)
    empty_value = jnp.zeros((), jnp.bfloat16)
    key_full, value_full = (
        lax.all_gather(key_weight, "seq", axis=1, tiled=True),
        lax.all_gather(value_weight, "seq", axis=1, tiled=True),
    )
    own_encoded, own_before, own_inverse = encode_rows(pool_flat, enc_gain, enc_up, enc_down)
    pieces = own_encoded.reshape(holding, neighbour_span, feature_width).reshape(
        holding, groups, piece_rows, feature_width
    )
    received = lax.all_to_all(pieces, "seq", split_axis=1, concat_axis=1, tiled=True)
    middle_rows = received.reshape(holding * groups, piece_rows, feature_width)[middle_index]
    gathered = lax.all_to_all(
        middle_rows.reshape(groups, stretch_count, piece_rows, feature_width),
        "seq",
        split_axis=0,
        concat_axis=2,
        tiled=True,
    )
    encoded_rows = gathered.reshape(stretch_count * neighbour_span, feature_width)
    head_count = key_full.shape[1] // HD
    score_scale = 1.0 / math.sqrt(HD)
    key_rows = jnp.dot(encoded_rows, key_full, preferred_element_type=jnp.float32).astype(
        jnp.bfloat16
    )
    value_rows = jnp.dot(encoded_rows, value_full, preferred_element_type=jnp.float32).astype(
        jnp.bfloat16
    )
    query_blocks = queries.reshape(stretch_count, STRETCH, head_count, HD)
    grad_blocks = attended_grad.reshape(stretch_count, STRETCH, head_count, HD)
    key_blocks = key_rows.reshape(stretch_count, neighbour_span, head_count, HD)
    value_blocks = value_rows.reshape(stretch_count, neighbour_span, head_count, HD)
    scores = (
        jnp.einsum("cqhe,ckhe->chqk", query_blocks, key_blocks, preferred_element_type=jnp.float32)
        * score_scale
    )
    exponent = jnp.exp(scores)
    weights = exponent / jnp.sum(exponent, axis=-1, keepdims=True)
    probabilities = weights.astype(jnp.bfloat16)
    attended = (
        jnp.einsum(
            "chqk,ckhe->cqhe", probabilities, value_blocks, preferred_element_type=jnp.float32
        )
        .astype(jnp.bfloat16)
        .reshape(queries.shape)
    )
    prob_grad = jnp.einsum(
        "cqhe,ckhe->chqk", grad_blocks, value_blocks, preferred_element_type=jnp.float32
    )
    score_grad = (
        weights * (prob_grad - jnp.sum(weights * prob_grad, axis=-1, keepdims=True)) * score_scale
    ).astype(jnp.bfloat16)
    query_grad = (
        jnp.einsum("chqk,ckhe->cqhe", score_grad, key_blocks, preferred_element_type=jnp.float32)
        .astype(jnp.bfloat16)
        .reshape(queries.shape)
    )
    key_grad = (
        jnp.einsum("chqk,cqhe->ckhe", score_grad, query_blocks, preferred_element_type=jnp.float32)
        .astype(jnp.bfloat16)
        .reshape(stretch_count * neighbour_span, -1)
    )
    value_grad = (
        jnp.einsum(
            "chqk,cqhe->ckhe", probabilities, grad_blocks, preferred_element_type=jnp.float32
        )
        .astype(jnp.bfloat16)
        .reshape(stretch_count * neighbour_span, -1)
    )
    key_part = jnp.einsum("rd,rh->dh", encoded_rows, key_grad, preferred_element_type=jnp.float32)
    value_part = jnp.einsum(
        "rd,rh->dh", encoded_rows, value_grad, preferred_element_type=jnp.float32
    )
    key_share, value_share = (
        lax.psum_scatter(
            key_part.astype(jnp.bfloat16), "seq", scatter_dimension=1, tiled=True
        ).astype(jnp.float32),
        lax.psum_scatter(
            value_part.astype(jnp.bfloat16), "seq", scatter_dimension=1, tiled=True
        ).astype(jnp.float32),
    )
    key_weight_grad, value_weight_grad = (
        lax.psum(key_share.astype(jnp.bfloat16), "dp").astype(jnp.float32),
        lax.psum(value_share.astype(jnp.bfloat16), "dp").astype(jnp.float32),
    )
    encoded_grad = (
        jnp.einsum("rh,dh->rd", key_grad, key_full, preferred_element_type=jnp.float32)
        + jnp.einsum("rh,dh->rd", value_grad, value_full, preferred_element_type=jnp.float32)
    ).astype(jnp.bfloat16)
    split_rows = lax.all_to_all(
        encoded_grad.reshape(1, stretch_count, neighbour_span, feature_width),
        "seq",
        split_axis=2,
        concat_axis=0,
        tiled=True,
    )
    middle_rows = split_rows.reshape(total_stretches, piece_rows, feature_width)
    placed = jnp.where(slot_named[:, None, None], middle_rows[slot_user], empty_value)
    returned = lax.all_to_all(
        placed.reshape(holding, groups, piece_rows, feature_width),
        "seq",
        split_axis=1,
        concat_axis=1,
        tiled=True,
    )
    slot_grad = returned.reshape(holding * neighbour_span, feature_width)
    pool_grad = encode_backward(
        slot_grad, pool_flat, own_before, own_inverse, enc_gain, enc_up, enc_down
    )
    return (
        attended,
        query_grad,
        pool_grad.reshape(1, holding, neighbour_span, feature_width),
        key_weight_grad,
        value_weight_grad,
    )


def solution(mesh):
    return jax.shard_map(
        on_device,
        mesh=mesh,
        in_specs=(
            P("dp", "seq", None),
            P("dp", "seq", None),
            P("dp", "seq", None, None),
            P("dp", None),
            P(),
            P(),
            P(),
            P(None, "seq"),
            P(None, "seq"),
        ),
        out_specs=(
            P("dp", "seq", None),
            P("dp", "seq", None),
            P("dp", "seq", None, None),
            P(None, "seq"),
            P(None, "seq"),
        ),
        check_vma=False,
    )
```

profile of v0, /device:TPU:1, one launch (start us, length us, event | category | flops | bytes accessed | tf_op | source)
XLA Modules:
  0.0 407.5 jit_solution(14458945438903055012)
XLA Ops:
  8.7 1.4 fusion.9
  10.1 1.5 fusion.11
  11.6 2.1 fusion.88
  13.8 2.3 fusion.12
  17.1 10.0 %all-to-all-start = ((bf16[4,16,8,896]{3,2,0,1:T(8,128)(2,1)}), bf16[4,16,8,896]{3,2,0,1:T(8,128)(2,1)}, u32[]{:S(2)}, u32[]{:S(2)}) async-start(bf16[4,16,8,896]{3,2,0,1:T(8,128)(2,1)} %copy.89), calls=%async_computation | async-start | bytes 1835008 | tf_op jit(solution)/shard_map/all_to_all | solution.py:86
  27.1 30.3 %all-to-all-done = bf16[4,16,8,896]{3,2,0,1:T(8,128)(2,1)} async-done(((bf16[4,16,8,896]{3,2,0,1:T(8,128)(2,1)}), bf16[4,16,8,896]{3,2,0,1:T(8,128)(2,1)}, u32[]{:S(2)}, u32[]{:S(2)}) %all-to-all-start) | async-done | bytes 917536 | tf_op jit(solution)/shard_map/all_to_all | solution.py:86
  57.4 2.2 copy.90
  59.6 2.5 gather_fusion
  62.1 4.1 %all-to-all-start.1 = ((bf16[16,2,8,896]{3,2,1,0:T(8,128)(2,1)}), bf16[16,2,8,896]{3,2,1,0:T(8,128)(2,1)}, u32[]{:S(2)}, u32[]{:S(2)}) async-start(bf16[16,2,8,896]{3,2,1,0:T(8,128)(2,1)} %bitcast.152), calls=%async_computation.1 | async-start | bytes 917504 | tf_op jit(solution)/shard_map/all_to_all | solution.py:88
  66.5 2.0 copy.115
  68.5 2.0 copy.117
  70.5 11.3 %all-to-all-done.1 = bf16[16,2,8,896]{3,2,1,0:T(8,128)(2,1)} async-done(((bf16[16,2,8,896]{3,2,1,0:T(8,128)(2,1)}), bf16[16,2,8,896]{3,2,1,0:T(8,128)(2,1)}, u32[]{:S(2)}, u32[]{:S(2)}) %all-to-all-start.1) | async-done | bytes 458784 | tf_op jit(solution)/shard_map/all_to_all | solution.py:88
  81.8 1.8 copy.91
  83.6 3.5 fusion.25
  88.3 42.9 %all-gather.5.cloned.1.call-done = bf16[896,2048]{1,0:T(8,128)(2,1)} async-done(((bf16[896,128]{1,0:T(8,128)(2,1)}), bf16[896,2048]{1,0:T(8,128)(2,1)}) %all-gather.5.cloned.1.call-update) | async-done | bytes 3670032 | tf_op jit(solution)/shard_map/all_gather | solution.py:79
  131.1 3.5 fusion.26
  135.9 1.4 fusion.56
  137.3 1.9 convolution_bitcast_fusion
  139.1 4.2 %fusion.23 = bf16[2,128,16,128]{3,1,2,0:T(8,128)(2,1)} fusion(f32[2,16,64,128]{3,2,1,0:T(8,128)} %fusion.56, f32[2,16,64,128]{3,2,1,0:T(8,128)} %convolution_bitcast_fusion, bf16[2,64,16,128]{3,2,1,0:T(8,128)(2,1)} %bitcast.136), kind=kOutput, calls=%fused_computation.38 | convolution fusion | flops 68946048 | bytes 3670016 | tf_op jit(solution)/shard_map/chqk,cqhe->ckhe/dot_general | solution.py:134
  143.3 1.9 copy.102
  146.2 4.0 convolution_convert_fusion.1
  150.2 6.1 %copy.110 = bf16[896,2048]{0,1:T(8,128)(2,1)} copy(bf16[896,2048]{1,0:T(8,128)(2,1)} %convolution_convert_fusion.1) | data formatting | bytes 7340032
  156.6 3.6 fusion.24
  160.1 1.9 copy.104
  163.0 4.0 convolution_convert_fusion
  167.0 6.1 %copy.112 = bf16[896,2048]{0,1:T(8,128)(2,1)} copy(bf16[896,2048]{1,0:T(8,128)(2,1)} %convolution_convert_fusion) | data formatting | bytes 7340032
  173.1 3.9 fusion.39
  179.6 4.4 %all-to-all-start.2 = ((bf16[1,2,128,896]{3,1,0,2:T(2,128)(2,1)}), bf16[1,2,128,896]{3,1,0,2:T(2,128)(2,1)}, u32[]{:S(2)}, u32[]{:S(2)}) async-start(bf16[1,2,128,896]{3,1,0,2:T(2,128)(2,1)} %copy.105), calls=%async_computation.2 | async-start | bytes 917504 | tf_op jit(solution)/shard_map/all_to_all | solution.py:165
  184.3 17.7 %all-to-all-done.2 = bf16[1,2,128,896]{3,1,0,2:T(2,128)(2,1)} async-done(((bf16[1,2,128,896]{3,1,0,2:T(2,128)(2,1)}), bf16[1,2,128,896]{3,1,0,2:T(2,128)(2,1)}, u32[]{:S(2)}, u32[]{:S(2)}) %all-to-all-start.2) | async-done | bytes 458784 | tf_op jit(solution)/shard_map/all_to_all | solution.py:165
  203.9 2.6 gather_fusion.1
  206.5 2.3 copy_select_fusion
  208.7 4.2 %all-to-all-start.3 = ((bf16[4,16,8,896]{3,2,0,1:T(8,128)(2,1)}), bf16[4,16,8,896]{3,2,0,1:T(8,128)(2,1)}, u32[]{:S(2)}, u32[]{:S(2)}) async-start(bf16[4,16,8,896]{3,2,0,1:T(8,128)(2,1)} %copy_select_fusion), calls=%async_computation.3 | async-start | bytes 1835008 | tf_op jit(solution)/shard_map/all_to_all | solution.py:174
  213.3 3.2 fusion.34
  216.5 2.2 copy.95
  218.7 2.1 reshape.248
  220.7 3.9 fusion.35
  224.7 2.2 copy.99
  226.8 2.1 reshape.250
  228.9 8.9 %all-to-all-done.3 = bf16[4,16,8,896]{3,2,0,1:T(8,128)(2,1)} async-done(((bf16[4,16,8,896]{3,2,0,1:T(8,128)(2,1)}), bf16[4,16,8,896]{3,2,0,1:T(8,128)(2,1)}, u32[]{:S(2)}, u32[]{:S(2)}) %all-to-all-start.3) | async-done | bytes 917536 | tf_op jit(solution)/shard_map/all_to_all | solution.py:174
  237.8 2.2 copy.109
  240.0 9.2 %fusion.16 = (f32[512]{0:T(512)S(1)}, f32[512,896]{1,0:T(8,128)}) fusion(bf16[1,4,128,896]{3,2,1,0:T(8,128)(2,1)} %param.11, f32[896]{0:T(1024)S(1)} %copy-done.10, bf16[896,1792]{1,0:T(8,128)(2,1)S(1)} %copy-done, f32[512,1792]{1,0:T(8,128)} %copy-done.14, bf16[512,896]{1,0:T(8,128)(2,1)} %bitcast.148, bf16[1792,896]{1,0:T(8,128)(2,1)} %param.15), kind=kOutput, calls=%fused_computation.30 | convolution fusion | flops 3308518912 | bytes 13768192 | tf_op jit(solution)/shard_map/rf,df->rd/dot_general | solution.py:33
  249.2 1.8 copy.111
  251.0 48.0 %reduce-scatter.9.cloned.1.call-done = bf16[128,896]{1,0:T(8,128)(2,1)} async-done(((bf16[2048,896]{1,0:T(8,128)(2,1)}), bf16[128,896]{1,0:T(8,128)(2,1)}) %reduce-scatter.9.cloned.1.call-update) | async-done | bytes 229392
  299.0 1.8 copy.113
  300.8 3.5 fusion.15
  304.3 93.1 %all-reduce.3.cloned.1.call-done = (bf16[896,128]{1,0:T(8,128)(2,1)}, bf16[896,128]{1,0:T(8,128)(2,1)}) async-done(((bf16[896,128]{1,0:T(8,128)(2,1)}, bf16[896,128]{1,0:T(8,128)(2,1)}), (bf16[896,128]{1,0:T(8,128)(2,1)}, bf16[896,128]{1,0:T(8,128)(2,1)})) %all-reduce.3.cloned.1.call-update) | async-done | bytes 458768 | tf_op jit(solution)/shard_map/psum | solution.py:158
  397.5 1.7 convert_element_type.106
  399.2 1.7 convert_element_type.108
  (62 shorter events, 12.7 us)
Async XLA Ops:
  7.2 4.4 %copy-start = (bf16[896,1792]{1,0:T(8,128)(2,1)S(1)}, bf16[896,1792]{1,0:T(8,128)(2,1)}, u32[]{:S(2)}) copy-start(bf16[896,1792]{1,0:T(8,128)(2,1)} %param.14) | copy-start | bytes 9633796
  7.2 76.4 %all-gather.3.cloned.1.call-start = ((), (), s32[]{:S(2)}) async-start(), calls=%async_computation.6 | async-start | bytes 3899392 | tf_op jit(solution)/shard_map/all_gather | solution.py:80
  7.9 123.2 %all-gather.5.cloned.1.call-start = ((), (), s32[]{:S(2)}) async-start(), calls=%async_computation.7 | async-start | bytes 3899392 | tf_op jit(solution)/shard_map/all_gather | solution.py:79
  11.6 2.1 copy-start.1
  11.6 2.2 copy-start.12
  13.8 2.3 copy-start.14
  16.1 11.0 %copy-start.13 = (s32[1,32]{1,0:T(1,128)S(1)}, s32[1,32]{1,0:T(1,128)}, u32[]{:S(2)}) copy-start(s32[1,32]{1,0:T(1,128)} %param.12) | copy-start | bytes 388
  17.1 40.3 %all-to-all-start = ((bf16[4,16,8,896]{3,2,0,1:T(8,128)(2,1)}), bf16[4,16,8,896]{3,2,0,1:T(8,128)(2,1)}, u32[]{:S(2)}, u32[]{:S(2)}) async-start(bf16[4,16,8,896]{3,2,0,1:T(8,128)(2,1)} %copy.89), calls=%async_computation | async-start | bytes 1835008 | tf_op jit(solution)/shard_map/all_to_all | solution.py:86
  62.1 19.6 %all-to-all-start.1 = ((bf16[16,2,8,896]{3,2,1,0:T(8,128)(2,1)}), bf16[16,2,8,896]{3,2,1,0:T(8,128)(2,1)}, u32[]{:S(2)}, u32[]{:S(2)}) async-start(bf16[16,2,8,896]{3,2,1,0:T(8,128)(2,1)} %bitcast.152), calls=%async_computation.1 | async-start | bytes 917504 | tf_op jit(solution)/shard_map/all_to_all | solution.py:88
  66.3 182.9 %reduce-scatter.7.cloned.1.call-start = ((), (), s32[]{:S(2)}) async-start(), calls=%async_computation.8 | async-start | bytes 3899392
  131.1 3.8 copy-start.2
  134.6 2.6 copy-start.4
  134.6 2.6 copy-start.8
  134.9 1.0 copy-start.3
  135.9 1.4 copy-start.9
  145.2 1.0 copy-start.5
  156.3 142.7 %reduce-scatter.9.cloned.1.call-start = ((), (), s32[]{:S(2)}) async-start(), calls=%async_computation.9 | async-start | bytes 3899392
  162.0 1.0 copy-start.6
  173.1 3.9 copy-start.7
  173.1 3.9 copy-start.11
  179.6 22.4 %all-to-all-start.2 = ((bf16[1,2,128,896]{3,1,0,2:T(2,128)(2,1)}), bf16[1,2,128,896]{3,1,0,2:T(2,128)(2,1)}, u32[]{:S(2)}, u32[]{:S(2)}) async-start(bf16[1,2,128,896]{3,1,0,2:T(2,128)(2,1)} %copy.105), calls=%async_computation.2 | async-start | bytes 917504 | tf_op jit(solution)/shard_map/all_to_all | solution.py:165
  208.7 29.0 %all-to-all-start.3 = ((bf16[4,16,8,896]{3,2,0,1:T(8,128)(2,1)}), bf16[4,16,8,896]{3,2,0,1:T(8,128)(2,1)}, u32[]{:S(2)}, u32[]{:S(2)}) async-start(bf16[4,16,8,896]{3,2,0,1:T(8,128)(2,1)} %copy_select_fusion), calls=%async_computation.3 | async-start | bytes 1835008 | tf_op jit(solution)/shard_map/all_to_all | solution.py:174
  213.0 184.5 %all-reduce.3.cloned.1.call-start = ((), (), s32[]{:S(2)}) async-start(), calls=%async_computation.10 | async-start | bytes 917504 | tf_op jit(solution)/shard_map/psum | solution.py:158
  218.7 21.3 %copy-start.10 = (f32[896]{0:T(1024)S(1)}, f32[896]{0:T(1024)}, u32[]{:S(2)}) copy-start(f32[896]{0:T(1024)} %param.13) | copy-start | bytes 10756
Sparse Core Ops, SparseCore 0:
  9.8 71.4 all-gather.2
  83.0 48.0 all-gather.4
  156.4 72.7 reduce-scatter.6
  231.6 67.3 reduce-scatter.8
  302.7 94.7 all-reduce.2
where the time goes:
time: 409 us; the launch traced here: 407 us
  waiting for transfers between devices  254 us (62%)
  local copies, waits for them, and re-layouts  51.3 us (13%)
  matrix products  51.2 us (13%)
  starting transfers between devices  23.6 us (6%)
  between operations  14.1 us (3%)
  other arithmetic  13.8 us (3%)
    psum x1, waiting for transfers between devices, on_device(): lax.psum(key_share.astype(jnp.bfloat16), 'dp').astype(jnp.float32)  93.1 us
    unnamed x7, waiting for transfers between devices  49.5 us
    all_gather x1, waiting for transfers between devices, on_device(): lax.all_gather(key_weight, 'seq', axis=1, tiled=True)  42.9 us
    all_to_all x1, waiting for transfers between devices, on_device(): lax.all_to_all(pieces, 'seq', split_axis=1, concat_axis=1, tiled=True)  30.3 us
    unnamed x38, local copies, waits for them, and re-layouts  23.3 us
    all_to_all x1, waiting for transfers between devices, on_device(): lax.all_to_all(encoded_grad.reshape(1, stretch_count, neighbour_span, fea...  17.7 us
    all_to_all x1, waiting for transfers between devices, on_device(): lax.all_to_all(middle_rows.reshape(groups, stretch_count, piece_rows, fea...  11.3 us
    all_to_all x1, starting transfers between devices, on_device(): lax.all_to_all(pieces, 'seq', split_axis=1, concat_axis=1, tiled=True)  9.97 us
  transfers between devices with their start and end apart: 9, of which 7 were waited for; matrix products, arithmetic and copies ran while one was open for 21% of the time, Pallas kernels for 0%

commit v1 on v0

v1 whole, which is shorter than its diff:
```python
import math

import jax
import jax.numpy as jnp
from jax import lax
from jax.experimental import pallas as pl
from jax.experimental.pallas import tpu as pltpu
from jax.sharding import PartitionSpec as P

STRETCH = 64
HD = 128
NX = 4
NZ = 8
CAP = 4
SLOTS = 64
NLEN = 128
PIECE = 16
DE = 896
FFE = 1792
HEADS = 16
WROWS = 448
WSUB = 112
TOKENS = 128
EPS = 1e-6
SCALE = 1.0 / math.sqrt(HD)

MESH = pl.DeviceIdType.MESH
BF16 = jnp.bfloat16
F32 = jnp.float32


class Place:
    def __init__(self):
        self.dp = lax.axis_index("dp")
        self.seq = lax.axis_index("seq")
        self.x = self.dp // NX
        self.y = self.dp % NX
        self.z = self.seq // 2
        self.c = self.seq % 2

    def xs(self, d):
        return (self.x + d + NX) % NX

    def ys(self, d):
        return (self.y + d + NX) % NX

    def zs(self, d):
        return (self.z + d + NZ) % NZ

    def at_x(self, d):
        return (self.xs(d) * NX + self.y, self.seq)

    def at_y(self, d):
        return (self.x * NX + self.ys(d), self.seq)

    def at_z(self, d):
        return (self.dp, self.zs(d) * 2 + self.c)

    def at_dp(self, d):
        return ((self.dp + d) % (NX * NX), self.seq)

    def sibling(self):
        return (self.dp, self.z * 2 + 1 - self.c)


def greet(partners):
    barrier = pltpu.get_barrier_semaphore()
    for partner in partners:
        pl.semaphore_signal(barrier, inc=1, device_id=partner, device_id_type=MESH)
    pl.semaphore_wait(barrier, len(partners))


class Copies:
    def __init__(self, send_sems, recv_sems):
        self.send_sems, self.recv_sems = send_sems, recv_sems
        self.count = 0
        self.all = []

    def start(self, src, dst, device):
        copy = pltpu.make_async_remote_copy(
            src_ref=src,
            dst_ref=dst,
            send_sem=self.send_sems.at[self.count],
            recv_sem=self.recv_sems.at[self.count],
            device_id=device,
            device_id_type=MESH,
        )
        self.count += 1
        self.all.append(copy)
        copy.start()
        return copy

    def finish(self):
        for copy in self.all:
            copy.wait_send()


def rows16(index):
    return pl.ds(pl.multiple_of(index * PIECE, PIECE), PIECE)


def sub(index):
    return pl.ds(pl.multiple_of(index * WSUB, 16), WSUB)


FRONT_COPIES = 56


def front_kernel(
    slot_ref, pool_ref, wk_ref, wv_ref, rows_ref, wall_ref, mid, out, ssem, rsem, lsem
):
    p = Place()
    z, c, x, y = p.z, p.c, p.x, p.y
    cp = Copies(ssem, rsem)

    def own_chunk(source):
        return pltpu.make_async_copy(
            source.at[x % 2, sub(y), :], wall_ref.at[z, c, x, sub(y), :], lsem.at[0]
        )

    @pl.when(x < 2)
    def key_chunk():
        own_chunk(wk_ref).start()

    @pl.when(x >= 2)
    def value_chunk():
        own_chunk(wv_ref).start()

    own_slots = pl.ds(p.seq * CAP, CAP)
    own_pool = pltpu.make_async_copy(pool_ref.at[:, rows16(z), :], mid.at[own_slots], lsem.at[2])
    own_pool.start()
    greet(
        [p.at_z(d) for d in range(1, NZ)]
        + [p.sibling(), p.at_x(1), p.at_x(-1), p.at_y(1), p.at_y(-1)]
    )

    own_chunk(wk_ref).wait()
    order = (4, 3, 5, 2, 6, 1, 7)

    def chunk(zz, xx, yy):
        return wall_ref.at[zz, c, xx, sub(yy), :]

    wz = [cp.start(chunk(z, x, y), chunk(z, x, y), p.at_z(d)) for d in order]
    hop1 = {
        d: cp.start(pool_ref.at[:, rows16(p.zs(d)), :], mid.at[own_slots], p.at_z(d))
        for d in order
    }
    forward = [cp.start(pool_ref.at[:, rows16(z), :], mid.at[own_slots], p.sibling())]

    for copy in wz:
        copy.wait_recv()
    lo, hi = pl.ds(0, 4), pl.ds(4, 4)

    def ring(region, first, places, at):
        src = region(first, places(0))
        return [cp.start(src, src, at(1)), cp.start(src, src, at(-1))]

    def ring2(region, first, places, at, arrived):
        arrived[0].wait_recv()
        src = region(pl.ds(first, 2), places(-1))
        one = cp.start(src, src, at(1))
        arrived[1].wait_recv()
        src = region(pl.ds(first + 2, 2), places(1))
        return [one, cp.start(src, src, at(-1))]

    def region_x(heads, xx):
        return wall_ref.at[heads, c, xx, sub(y), :]

    def region_y(heads, yy):
        return wall_ref.at[heads, c, x, sub(yy), :]

    def wide_y(heads, yy):
        return wall_ref.at[heads, c, :, sub(yy), :]

    def wide_x(heads, xx):
        return wall_ref.at[heads, c, xx, :, :]

    a1 = ring(region_x, lo, p.xs, p.at_x)
    b1 = ring(region_y, hi, p.ys, p.at_y)
    a2 = ring2(region_x, 0, p.xs, p.at_x, a1)
    b2 = ring2(region_y, 4, p.ys, p.at_y, b1)
    for copy in a2:
        copy.wait_recv()
    a3 = ring(wide_y, lo, p.ys, p.at_y)
    for copy in b2:
        copy.wait_recv()
    b3 = ring(wide_x, hi, p.xs, p.at_x)
    sib = []

    def share(src):
        sib.append(cp.start(src, src, p.sibling()))

    share(wide_y(lo, y))
    share(wide_x(hi, x))

    own_pool.wait()
    for d in (1, 7, 2, 6, 3, 5, 4):
        hop1[d].wait_recv()
        block = mid.at[pl.ds((p.zs(-d) * 2 + c) * CAP, CAP)]
        forward.append(cp.start(block, block, p.sibling()))
    for copy in forward:
        copy.wait_recv()
    hop2 = []
    for d in order + (0,):
        target = p.zs(d) * 2 + c
        for i in range(2):
            out[d, i] = mid[slot_ref[target * 2 + i]]
        dst = rows_ref.at[:, rows16(z), :]
        if d == 0:
            own_rows = pltpu.make_async_copy(out.at[d], dst, lsem.at[3])
            own_rows.start()
        else:
            hop2.append(cp.start(out.at[d], dst, p.at_z(d)))

    a4 = ring2(wide_y, 0, p.ys, p.at_y, a3)
    b4 = ring2(wide_x, 4, p.xs, p.at_x, b3)
    share(wide_y(lo, p.ys(1)))
    share(wide_y(lo, p.ys(-1)))
    share(wide_x(hi, p.xs(1)))
    share(wide_x(hi, p.xs(-1)))
    a4[0].wait_recv()
    share(wide_y(pl.ds(0, 2), p.ys(2)))
    a4[1].wait_recv()
    share(wide_y(pl.ds(2, 2), p.ys(2)))
    b4[0].wait_recv()
    share(wide_x(pl.ds(4, 2), p.xs(2)))
    b4[1].wait_recv()
    share(wide_x(pl.ds(6, 2), p.xs(2)))
    own_rows.wait()
    for copy in hop2 + sib:
        copy.wait_recv()
    cp.finish()


def front(slots, pool, wk, wv):
    anyspace = pl.BlockSpec(memory_space=pl.ANY)
    return pl.pallas_call(
        front_kernel,
        out_shape=(
            jax.ShapeDtypeStruct((2, NLEN, DE), BF16),
            jax.ShapeDtypeStruct((NZ, 2, 4, WROWS, HD), BF16),
        ),
        in_specs=[pl.BlockSpec(memory_space=pltpu.SMEM), anyspace, anyspace, anyspace],
        out_specs=(anyspace, anyspace),
        scratch_shapes=[
            pltpu.VMEM((SLOTS, PIECE, DE), BF16),
            pltpu.VMEM((NZ, 2, PIECE, DE), BF16),
            pltpu.SemaphoreType.DMA((FRONT_COPIES,)),
            pltpu.SemaphoreType.DMA((FRONT_COPIES,)),
            pltpu.SemaphoreType.DMA((4,)),
        ],
        compiler_params=pltpu.CompilerParams(
            collective_id=0, has_side_effects=True, vmem_limit_bytes=16 * 1024 * 1024
        ),
        name="front",
    )(slots, pool, wk, wv)


def dot(a, b):
    return jnp.dot(a, b, preferred_element_type=F32)


def dot_nt(a, b):
    return lax.dot_general(a, b, (((1,), (1,)), ((), ())), preferred_element_type=F32)


def dot_tn(a, b):
    return lax.dot_general(a, b, (((0,), (0,)), ((), ())), preferred_element_type=F32)


def core_kernel(
    rows_ref, gain_ref, up_ref, down_ref, w_ref, q_ref, g_ref,
    att_ref, qg_ref, pg_ref, wg_ref,
    enc_ref, enct_ref, slope_ref, inv_ref, acc_ref,
):
    head = pl.program_id(0)
    root = math.sqrt(2.0 / math.pi)
    tile = 256

    @pl.when(head == 0)
    def encode():
        rows = rows_ref[...].astype(F32)
        inverse = lax.rsqrt(jnp.mean(rows * rows, axis=-1, keepdims=True) + EPS)
        inv_ref[...] = inverse
        normed = (rows * inverse * gain_ref[...]).astype(BF16)
        total = rows
        for t in range(FFE // tile):
            span = slice(t * tile, (t + 1) * tile)
            before = dot(normed, up_ref[:, span])
            square = before * before
            th = jnp.tanh(root * before * (1.0 + 0.044715 * square))
            half = 0.5 * (1.0 + th)
            slope_ref[:, span] = half + 0.5 * before * (1.0 - th * th) * root * (
                1.0 + 3.0 * 0.044715 * square
            )
            total = total + dot((before * half).astype(BF16), down_ref[span, :])
        encoded = total.astype(BF16)
        enc_ref[...] = encoded
        enct_ref[...] = encoded.T
        acc_ref[...] = jnp.zeros_like(acc_ref)

    w = jnp.concatenate([w_ref[0, 0], w_ref[0, 1]], axis=1)
    kv = dot(enc_ref[...], w).astype(BF16)
    kv_grads = []
    for i in range(2):
        tokens = slice(i * STRETCH, (i + 1) * STRETCH)
        k = kv[i * NLEN : (i + 1) * NLEN, :HD]
        v = kv[i * NLEN : (i + 1) * NLEN, HD:]
        q, g = q_ref[tokens, :], g_ref[tokens, :]
        exponent = jnp.exp(dot_nt(q, k) * SCALE)
        weights = exponent / jnp.sum(exponent, axis=-1, keepdims=True)
        probs = weights.astype(BF16)
        att_ref[tokens, :] = dot(probs, v).astype(BF16)
        prob_grad = dot_nt(g, v)
        mean = jnp.sum(weights * prob_grad, axis=-1, keepdims=True)
        score_grad = (weights * (prob_grad - mean) * SCALE).astype(BF16)
        qg_ref[tokens, :] = dot(score_grad, k).astype(BF16)
        kv_grads.append(
            jnp.concatenate([dot_tn(score_grad, q), dot_tn(probs, g)], axis=1).astype(BF16)
        )
    kv_grad = jnp.concatenate(kv_grads, axis=0)
    part = dot(enct_ref[...], kv_grad).astype(BF16)
    wg_ref[0, 0] = part[:, :HD]
    wg_ref[0, 1] = part[:, HD:]
    acc_ref[...] += dot_nt(kv_grad, w)

    @pl.when(head == HEADS - 1)
    def encode_back():
        encoded_grad = acc_ref[...].astype(BF16)
        normed_grad = jnp.zeros((2 * NLEN, DE), F32)
        for t in range(FFE // tile):
            span = slice(t * tile, (t + 1) * tile)
            before_grad = (dot_nt(encoded_grad, down_ref[span, :]) * slope_ref[:, span]).astype(BF16)
            normed_grad = normed_grad + dot_nt(before_grad, up_ref[:, span])
        rows = rows_ref[...].astype(F32)
        inverse = inv_ref[...]
        scaled = gain_ref[...] * normed_grad
        result = (
            encoded_grad.astype(F32)
            + inverse * scaled
            - rows
            * (inverse * inverse * inverse)
            * jnp.mean(rows * scaled, axis=-1, keepdims=True)
        )
        pg_ref[...] = result.astype(BF16)


def core(rows, gain, up, down, wall, queries, grads):
    whole = pl.BlockSpec(memory_space=pltpu.VMEM)
    column = pl.BlockSpec((TOKENS, HD), lambda h: (0, h))
    block = pl.BlockSpec((1, 2, DE, HD), lambda h: (h, 0, 0, 0))
    r = 2 * NLEN
    return pl.pallas_call(
        core_kernel,
        grid=(HEADS,),
        out_shape=(
            jax.ShapeDtypeStruct((TOKENS, HEADS * HD), BF16),
            jax.ShapeDtypeStruct((TOKENS, HEADS * HD), BF16),
            jax.ShapeDtypeStruct((r, DE), BF16),
            jax.ShapeDtypeStruct((HEADS, 2, DE, HD), BF16),
        ),
        in_specs=[whole, whole, whole, whole, block, column, column],
        out_specs=(column, column, pl.BlockSpec((r, DE), lambda h: (0, 0)), block),
        scratch_shapes=[
            pltpu.VMEM((r, DE), BF16),
            pltpu.VMEM((DE, r), BF16),
            pltpu.VMEM((r, FFE), F32),
            pltpu.VMEM((r, 1), F32),
            pltpu.VMEM((r, DE), F32),
        ],
        compiler_params=pltpu.CompilerParams(
            dimension_semantics=("arbitrary",), vmem_limit_bytes=48 * 1024 * 1024
        ),
        name="core",
    )(rows, gain, up, down, wall, queries, grads)


BACK_COPIES = 72


def back_kernel(
    user_ref, pg_ref, wg_ref, pool_ref, kw_ref, vw_ref,
    part, other, mid, out, ya1, ya2, xa1, xa2, xb1, xb2, yb1, yb2, zbuf, fin, ssem, rsem, lsem,
):
    p = Place()
    z, c, x, y = p.z, p.c, p.x, p.y
    cp = Copies(ssem, rsem)
    own_two = pl.ds(p.seq * 2 + 1, 2)
    own_mid = pltpu.make_async_copy(pg_ref.at[:, rows16(z), :], mid.at[own_two], lsem.at[0])
    own_mid.start()
    own_part = pltpu.make_async_copy(wg_ref.at[:, c], part, lsem.at[1])
    own_part.start()
    greet(
        [p.at_z(d) for d in range(1, NZ)] + [p.sibling()] + [p.at_dp(d) for d in range(1, NX * NX)]
    )
    order = (4, 3, 5, 2, 6, 1, 7)
    forward = [cp.start(pg_ref.at[:, rows16(z), :], mid.at[own_two], p.sibling())]
    hop1 = {
        d: cp.start(pg_ref.at[:, rows16(p.zs(d)), :], mid.at[own_two], p.at_z(d)) for d in order
    }
    sib = [cp.start(wg_ref.at[h, 1 - c], other.at[h], p.sibling()) for h in range(NZ)]
    mid[0] = jnp.zeros((PIECE, DE), BF16)
    own_part.wait()

    def add_sibling(h):
        sib[h].wait_recv()

        def body(i, carry):
            part[h, i] = (part[h, i].astype(F32) + other[h, i].astype(F32)).astype(BF16)
            return carry

        lax.fori_loop(0, 4, body, 0)

    def wide_y(first, count, yy):
        return part.at[pl.ds(first, count), :, sub(yy), :]

    def wide_x(first, count, xx):
        return part.at[pl.ds(first, count), xx, :, :]

    def region_x(first, count, xx):
        return part.at[pl.ds(first, count), xx, sub(y), :]

    def region_y(first, count, yy):
        return part.at[pl.ds(first, count), x, sub(yy), :]

    def far(region, first, places, at, land):
        return [
            cp.start(region(first, 2, places(2)), land.at[0], at(1)),
            cp.start(region(first + 2, 2, places(2)), land.at[1], at(-1)),
        ]

    def near(region, first, places, at, arrived, land1, land2):
        sent = []
        for side, d in ((0, 1), (1, -1)):
            arrived[side].wait_recv()
            block = region(first + 2 * side, 2, places(d))
            block[...] = (block[...].astype(F32) + land1[side].astype(F32)).astype(BF16)
            sent.append(cp.start(region(first, 4, places(d)), land2.at[side], at(d)))
        return sent

    def close(region, first, places, arrived, land2):
        for copy in arrived:
            copy.wait_recv()
        block = region(first, 4, places(0))
        block[...] = (
            block[...].astype(F32) + land2[0].astype(F32) + land2[1].astype(F32)
        ).astype(BF16)

    for h in range(4):
        add_sibling(h)
    a1 = far(wide_y, 0, p.ys, p.at_y, ya1)
    for h in range(4, NZ):
        add_sibling(h)
    b1 = far(wide_x, 4, p.xs, p.at_x, xb1)

    for d in (1, 7, 2, 6, 3, 5, 4):
        hop1[d].wait_recv()
        block = mid.at[pl.ds((p.zs(-d) * 2 + c) * 2 + 1, 2)]
        forward.append(cp.start(block, block, p.sibling()))
    a2 = near(wide_y, 0, p.ys, p.at_y, a1, ya1, ya2)
    b2 = near(wide_x, 4, p.xs, p.at_x, b1, xb1, xb2)
    own_mid.wait()
    for copy in forward:
        copy.wait_recv()
    hop2 = []
    for d in order + (0,):
        target = p.zs(d) * 2 + c
        for j in range(CAP):
            out[d, j] = mid[user_ref[target * CAP + j]]
        dst = pool_ref.at[:, rows16(z), :]
        if d == 0:
            own_rows = pltpu.make_async_copy(out.at[d], dst, lsem.at[2])
            own_rows.start()
        else:
            hop2.append(cp.start(out.at[d], dst, p.at_z(d)))

    close(wide_y, 0, p.ys, a2, ya2)
    a3 = far(region_x, 0, p.xs, p.at_x, xa1)
    close(wide_x, 4, p.xs, b2, xb2)
    b3 = far(region_y, 4, p.ys, p.at_y, yb1)
    a4 = near(region_x, 0, p.xs, p.at_x, a3, xa1, xa2)
    b4 = near(region_y, 4, p.ys, p.at_y, b3, yb1, yb2)
    close(region_x, 0, p.xs, a4, xa2)
    close(region_y, 4, p.ys, b4, yb2)
    zsum = [cp.start(part.at[p.zs(d), x, sub(y), :], zbuf.at[d], p.at_z(d)) for d in order]
    for copy in zsum:
        copy.wait_recv()
    total = part[z, x, sub(y), :].astype(F32)
    for d in range(1, NZ):
        total = total + zbuf[d].astype(F32)
    fin[x, y] = total.astype(BF16)
    last = [cp.start(fin.at[x, y], fin.at[x, y], p.at_dp(d)) for d in range(1, NX * NX)]
    for copy in last:
        copy.wait_recv()
    for xx in range(2):
        for yy in range(NX):
            span = slice(xx * WROWS + yy * WSUB, xx * WROWS + (yy + 1) * WSUB)
            kw_ref[span, :] = fin[xx, yy].astype(F32)
            vw_ref[span, :] = fin[xx + 2, yy].astype(F32)
    own_rows.wait()
    for copy in hop2:
        copy.wait_recv()
    cp.finish()


def back(user, pool_rows, wgrads):
    anyspace = pl.BlockSpec(memory_space=pl.ANY)
    whole = pl.BlockSpec(memory_space=pltpu.VMEM)
    return pl.pallas_call(
        back_kernel,
        out_shape=(
            jax.ShapeDtypeStruct((CAP, NLEN, DE), BF16),
            jax.ShapeDtypeStruct((DE, HD), F32),
            jax.ShapeDtypeStruct((DE, HD), F32),
        ),
        in_specs=[pl.BlockSpec(memory_space=pltpu.SMEM), anyspace, anyspace],
        out_specs=(anyspace, whole, whole),
        scratch_shapes=[
            pltpu.VMEM((NZ, 4, WROWS, HD), BF16),
            pltpu.VMEM((NZ, 4, WROWS, HD), BF16),
            pltpu.VMEM((1 + SLOTS // 2, PIECE, DE), BF16),
            pltpu.VMEM((NZ, CAP, PIECE, DE), BF16),
            pltpu.VMEM((2, 2, 4, WSUB, HD), BF16),
            pltpu.VMEM((2, 4, 4, WSUB, HD), BF16),
            pltpu.VMEM((2, 2, WSUB, HD), BF16),
            pltpu.VMEM((2, 4, WSUB, HD), BF16),
            pltpu.VMEM((2, 2, WROWS, HD), BF16),
            pltpu.VMEM((2, 4, WROWS, HD), BF16),
            pltpu.VMEM((2, 2, WSUB, HD), BF16),
            pltpu.VMEM((2, 4, WSUB, HD), BF16),
            pltpu.VMEM((NZ, WSUB, HD), BF16),
            pltpu.VMEM((NX, NX, WSUB, HD), BF16),
            pltpu.SemaphoreType.DMA((BACK_COPIES,)),
            pltpu.SemaphoreType.DMA((BACK_COPIES,)),
            pltpu.SemaphoreType.DMA((3,)),
        ],
        compiler_params=pltpu.CompilerParams(
            collective_id=1, has_side_effects=True, vmem_limit_bytes=32 * 1024 * 1024
        ),
        name="back",
    )(user, pool_rows, wgrads)


def on_device(queries, attended_grad, pool, stretch_slot, gain, up, down, key_w, value_w):
    slots = stretch_slot[0]
    match = slots[:, None] == jnp.arange(SLOTS, dtype=jnp.int32)[None, :]
    place = jnp.arange(1, slots.shape[0] + 1, dtype=jnp.int32)[:, None]
    user = jnp.sum(jnp.where(match, place, 0), axis=0)
    rows, wall = front(slots, pool[0], key_w.reshape(2, WROWS, HD), value_w.reshape(2, WROWS, HD))
    attended, query_grad, pool_rows, wgrads = core(
        rows.reshape(2 * NLEN, DE),
        gain.reshape(1, DE),
        up,
        down,
        wall.reshape(HEADS, 2, DE, HD),
        queries[0],
        attended_grad[0],
    )
    pool_grad, key_grad, value_grad = back(
        user, pool_rows.reshape(2, NLEN, DE), wgrads.reshape(NZ, 2, 4, WROWS, HD)
    )
    return attended[None], query_grad[None], pool_grad[None], key_grad, value_grad


def solution(mesh):
    return jax.shard_map(
        on_device,
        mesh=mesh,
        in_specs=(
            P("dp", "seq", None),
            P("dp", "seq", None),
            P("dp", "seq", None, None),
            P("dp", None),
            P(),
            P(),
            P(),
            P(None, "seq"),
            P(None, "seq"),
        ),
        out_specs=(
            P("dp", "seq", None),
            P("dp", "seq", None),
            P("dp", "seq", None, None),
            P(None, "seq"),
            P(None, "seq"),
        ),
        check_vma=False,
    )
```

time: 409 us -> 165 us (0.40)
  waiting for transfers between devices: 254 us -> 0 us
  Pallas kernels: 0 us -> 146 us
  matrix products: 51.2 us -> 0 us
  local copies, waits for them, and re-layouts: 51.3 us -> 16.9 us
  starting transfers between devices: 23.6 us -> 0 us
  other arithmetic: 13.8 us -> 0.1 us
  between operations: 14.1 us -> 0.68 us
    pallas_call x0 -> x3, Pallas kernels: none -> 146 us  [the longest x1 54 us: back(): pl.pallas_call(back_kernel, out_shape=(jax.ShapeDtypeStruct((CAP, NLEN, D...]
    psum x1 -> x0, waiting for transfers between devices: 93.1 us -> none  [on_device(): lax.psum(key_share.astype(jnp.bfloat16), 'dp').astype(jnp.float32)]
    all_to_all x4 -> x0, waiting for transfers between devices: 68.1 us -> none  [the longest x1 30.3 us: on_device(): lax.all_to_all(pieces, 'seq', split_axis=1, concat_axis=1, tiled=True)]
    dot_general x15 -> x0, matrix products: 51.2 us -> none  [the longest x1 9.22 us: encode_backward(): jnp.einsum('rf,df->rd', before_grad, up_matrix, preferred_element_type=jn...]
    unnamed x7 -> x0, waiting for transfers between devices: 49.5 us -> none
    all_gather x2 -> x0, waiting for transfers between devices: 42.9 us -> none  [the longest x1 42.9 us: on_device(): lax.all_gather(key_weight, 'seq', axis=1, tiled=True)]
    all_to_all x4 -> x0, starting transfers between devices: 22.7 us -> none  [the longest x1 9.97 us: on_device(): lax.all_to_all(pieces, 'seq', split_axis=1, concat_axis=1, tiled=True)]
    convert_element_type x4 -> x0, other arithmetic: 8.44 us -> none  [the longest x1 3.5 us: encode_backward(): return result.astype(jnp.bfloat16)]
  transfers between devices with their start and end apart: 9 -> 0, of which waited for: 7 -> 0; matrix products, arithmetic and copies ran while one was open for 21% -> 0% of each run, Pallas kernels for 0% -> 0%
where the time goes in v1:
time: 165 us; the launch traced here: 164 us
  Pallas kernels  146 us (88%)
  local copies, waits for them, and re-layouts  16.9 us (10%)
    pallas_call x1, Pallas kernels, back(): pl.pallas_call(back_kernel, out_shape=(jax.ShapeDtypeStruct((CAP, NLEN, D...  54 us
    pallas_call x1, Pallas kernels, front(): pl.pallas_call(front_kernel, out_shape=(jax.ShapeDtypeStruct((2, NLEN, DE...  50.7 us
    pallas_call x1, Pallas kernels, core(): pl.pallas_call(core_kernel, grid=(HEADS,), out_shape=(jax.ShapeDtypeStruc...  41.7 us
    unnamed x23, local copies, waits for them, and re-layouts  16.2 us

profile of v1, /device:TPU:1, one launch (start us, length us, event | category | flops | bytes accessed | tf_op | source)
XLA Modules:
  0.0 164.0 jit_solution(9737083284886286876)
XLA Ops:
  0.6 0.0 copy-start.3
  0.6 1.2 copy-done.3
  1.8 0.0 copy-start.6
  1.8 0.9 copy-done.6
  2.8 0.0 copy-start.7
  2.8 0.9 copy-done.7
  3.7 0.0 copy-start.8
  3.7 0.7 copy-done.8
  4.3 50.7 %front.1 = (bf16[2,128,896]{2,1,0:T(8,128)(2,1)S(1)}, bf16[8,2,4,448,128]{4,3,2,1,0:T(8,128)(2,1)S(1)}) custom-call(s32[32]{0:T(128)S(1)} %bitcast.23, bf16[4,128,896]{2,1,0:T(8,128)(2,1)S(1)} %bitcast.15, bf16[2,448,128]{2,1,0:T(8,128)(2,1)S(1)} %bitcast.21, bf16[2,448,128]{2,1,0:T(8,128)(2,1)S(1)} %bitcast.22), custom_call_target="tpu_custom_call" | custom-call | tf_op jit(solution)/shard_map/front/pallas_call | solution.py:237
  55.0 0.0 copy-start
  55.0 2.9 %copy-done = bf16[8,2,4,448,128]{4,3,2,1,0:T(8,128)(2,1)} copy-done((bf16[8,2,4,448,128]{4,3,2,1,0:T(8,128)(2,1)}, bf16[8,2,4,448,128]{4,3,2,1,0:T(8,128)(2,1)S(1)}, u32[]{:S(2)}) %copy-start) | copy-done | bytes 7340056
  57.9 0.7 reshape.39.gain_ref
  58.6 0.0 copy-start.2
  58.6 1.9 %copy-done.2 = bf16[896,1792]{1,0:T(8,128)(2,1)S(1)} copy-done((bf16[896,1792]{1,0:T(8,128)(2,1)S(1)}, bf16[896,1792]{1,0:T(8,128)(2,1)}, u32[]{:S(2)}) %copy-start.2) | copy-done | bytes 3211288
  60.5 0.0 copy-start.4
  60.5 1.0 copy-done.4
  61.6 0.0 copy-start.5
  61.6 1.0 copy-done.5
  62.6 0.0 copy-start.9
  62.6 41.7 %core.1 = (bf16[128,2048]{1,0:T(8,128)(2,1)}, bf16[128,2048]{1,0:T(8,128)(2,1)}, bf16[256,896]{1,0:T(8,128)(2,1)S(1)}, bf16[16,2,896,128]{3,2,1,0:T(8,128)(2,1)}) custom-call(bf16[256,896]{1,0:T(8,128)(2,1)S(1)} %bitcast.20, f32[1,896]{1,0:T(1,128)S(1)} %reshape.39.gain_ref, bf16[896,1792]{1,0:T(8,128)(2,1)S(1)} %copy-done.2, bf16[1792,896]{1,0:T(8,128)(2,1)} %down_ref.1, ...), custom_call_target="tpu_custom_call" | custom-call | tf_op jit(solution)/shard_map/core/pallas_call | solution.py:353
  104.3 0.0 copy-done.9
  104.3 0.1 select_reduce_fusion.user_ref
  104.4 0.0 copy-start.1
  104.4 3.1 %copy-done.1 = bf16[16,2,896,128]{3,2,1,0:T(8,128)(2,1)S(1)} copy-done((bf16[16,2,896,128]{3,2,1,0:T(8,128)(2,1)S(1)}, bf16[16,2,896,128]{3,2,1,0:T(8,128)(2,1)}, u32[]{:S(2)}) %copy-start.1) | copy-done | bytes 7340056
  107.5 54.0 %back.1 = (bf16[4,128,896]{2,1,0:T(8,128)(2,1)S(1)}, f32[896,128]{1,0:T(8,128)S(1)}, f32[896,128]{1,0:T(8,128)S(1)}) custom-call(s32[64]{0:T(128)S(1)} %select_reduce_fusion.user_ref, bf16[2,128,896]{2,1,0:T(8,128)(2,1)S(1)} %bitcast.19, bf16[8,2,4,448,128]{4,3,2,1,0:T(8,128)(2,1)S(1)} %bitcast.14), custom_call_target="tpu_custom_call" | custom-call | tf_op jit(solution)/shard_map/back/pallas_call | solution.py:509
  161.5 0.9 copy.17
  162.5 0.8 copy.18
  163.2 0.8 copy.19
  (1 shorter events, 0.0 us)
Async XLA Ops:
  0.6 1.2 copy-start.3
  1.8 0.9 copy-start.6
  2.8 0.9 copy-start.7
  3.7 0.7 copy-start.8
  55.0 2.9 %copy-start = (bf16[8,2,4,448,128]{4,3,2,1,0:T(8,128)(2,1)}, bf16[8,2,4,448,128]{4,3,2,1,0:T(8,128)(2,1)S(1)}, u32[]{:S(2)}) copy-start(bf16[8,2,4,448,128]{4,3,2,1,0:T(8,128)(2,1)S(1)} %get-tuple-element.15) | copy-start | bytes 22020100
  58.6 1.9 %copy-start.2 = (bf16[896,1792]{1,0:T(8,128)(2,1)S(1)}, bf16[896,1792]{1,0:T(8,128)(2,1)}, u32[]{:S(2)}) copy-start(bf16[896,1792]{1,0:T(8,128)(2,1)} %up_ref.1) | copy-start | bytes 9633796
  60.5 1.0 copy-start.4
  61.6 1.0 copy-start.5
  62.6 41.7 %copy-start.9 = (s32[1,32]{1,0:T(1,128)S(1)}, s32[1,32]{1,0:T(1,128)}, u32[]{:S(2)}) copy-start(s32[1,32]{1,0:T(1,128)} %param.12) | copy-start | bytes 388
  104.4 3.1 %copy-start.1 = (bf16[16,2,896,128]{3,2,1,0:T(8,128)(2,1)S(1)}, bf16[16,2,896,128]{3,2,1,0:T(8,128)(2,1)}, u32[]{:S(2)}) copy-start(bf16[16,2,896,128]{3,2,1,0:T(8,128)(2,1)} %get-tuple-element.19) | copy-start | bytes 22020100

commit v2 on v1

v2 whole, which is shorter than its diff:
```python
import math

import jax
import jax.numpy as jnp
from jax import lax
from jax.experimental import pallas as pl
from jax.experimental.pallas import tpu as pltpu
from jax.sharding import PartitionSpec as P

STRETCH = 64
HD = 128
NX = 4
NZ = 8
CAP = 4
SLOTS = 64
NLEN = 128
PIECE = 16
DE = 896
FFE = 1792
HEADS = 16
WROWS = 448
WSUB = 112
TOKENS = 128
EPS = 1e-6
SCALE = 1.0 / math.sqrt(HD)

MESH = pl.DeviceIdType.MESH
BF16 = jnp.bfloat16
F32 = jnp.float32


class Place:
    def __init__(self):
        self.dp = lax.axis_index("dp")
        self.seq = lax.axis_index("seq")
        self.x = self.dp // NX
        self.y = self.dp % NX
        self.z = self.seq // 2
        self.c = self.seq % 2

    def xs(self, d):
        return (self.x + d + NX) % NX

    def ys(self, d):
        return (self.y + d + NX) % NX

    def zs(self, d):
        return (self.z + d + NZ) % NZ

    def at_x(self, d):
        return (self.xs(d) * NX + self.y, self.seq)

    def at_y(self, d):
        return (self.x * NX + self.ys(d), self.seq)

    def at_z(self, d):
        return (self.dp, self.zs(d) * 2 + self.c)

    def at_dp(self, d):
        return ((self.dp + d) % (NX * NX), self.seq)

    def sibling(self):
        return (self.dp, self.z * 2 + 1 - self.c)


def greet(partners):
    barrier = pltpu.get_barrier_semaphore()
    for partner in partners:
        pl.semaphore_signal(barrier, inc=1, device_id=partner, device_id_type=MESH)
    pl.semaphore_wait(barrier, len(partners))


class Copies:
    def __init__(self, send_sems, recv_sems):
        self.send_sems, self.recv_sems = send_sems, recv_sems
        self.count = 0
        self.all = []

    def start(self, src, dst, device):
        copy = pltpu.make_async_remote_copy(
            src_ref=src,
            dst_ref=dst,
            send_sem=self.send_sems.at[self.count],
            recv_sem=self.recv_sems.at[self.count],
            device_id=device,
            device_id_type=MESH,
        )
        self.count += 1
        self.all.append(copy)
        copy.start()
        return copy

    def finish(self):
        for copy in self.all:
            copy.wait_send()


def rows16(index):
    return pl.ds(pl.multiple_of(index * PIECE, PIECE), PIECE)


def sub(index):
    return pl.ds(pl.multiple_of(index * WSUB, 16), WSUB)


COPIES = 136
GROUP = 8
TILE = 256
ROWS = 2 * NLEN


def dot(a, b):
    return jnp.dot(a, b, preferred_element_type=F32)


def dot_nt(a, b):
    return lax.dot_general(a, b, (((1,), (1,)), ((), ())), preferred_element_type=F32)


def dot_tn(a, b):
    return lax.dot_general(a, b, (((0,), (0,)), ((), ())), preferred_element_type=F32)


def encode(rows_ref, gain_ref, up, down, slope, inv):
    rows = rows_ref[...].reshape(ROWS, DE).astype(F32)
    inverse = lax.rsqrt(jnp.mean(rows * rows, axis=-1, keepdims=True) + EPS)
    inv[...] = inverse
    normed = (rows * inverse * gain_ref[...]).astype(BF16)
    root = math.sqrt(2.0 / math.pi)
    before = dot(normed, up[...])
    square = before * before
    th = jnp.tanh(root * before * (1.0 + 0.044715 * square))
    half = 0.5 * (1.0 + th)
    slope[...] = half + 0.5 * before * (1.0 - th * th) * root * (1.0 + 3.0 * 0.044715 * square)
    return (rows + dot((before * half).astype(BF16), down[...])).astype(BF16)


def encode_back(encoded_grad, rows_ref, gain_ref, up, down, slope, inv):
    before_grad = (dot_nt(encoded_grad, down[...]) * slope[...]).astype(BF16)
    normed_grad = dot_nt(before_grad, up[...])
    rows = rows_ref[...].reshape(ROWS, DE).astype(F32)
    inverse = inv[...]
    scaled = gain_ref[...] * normed_grad
    result = (
        encoded_grad.astype(F32)
        + inverse * scaled
        - rows
        * (inverse * inverse * inverse)
        * jnp.mean(rows * scaled, axis=-1, keepdims=True)
    )
    return result.astype(BF16)


def attention(first, count, q_all, g_all, kv, kvg, att, qg):
    zero = jnp.zeros((STRETCH, HD), BF16)
    units = [(h, i) for h in range(first, first + count) for i in range(2)]
    pairs, products, mixes = [], [], []
    for h, i in units:
        column, tokens = slice(h * HD, (h + 1) * HD), slice(i * STRETCH, (i + 1) * STRETCH)
        pair = jnp.concatenate(
            [
                jnp.concatenate([q_all[tokens, column], zero], axis=1),
                jnp.concatenate([zero, g_all[tokens, column]], axis=1),
            ],
            axis=0,
        )
        pairs.append(pair)
        products.append(dot_nt(pair, kv[h // 2, h % 2, i * NLEN : (i + 1) * NLEN, :]))
    for product in products:
        exponent = jnp.exp(product[:STRETCH] * SCALE)
        weights = exponent / jnp.sum(exponent, axis=-1, keepdims=True)
        prob_grad = product[STRETCH:]
        mean = jnp.sum(weights * prob_grad, axis=-1, keepdims=True)
        score_grad = weights * (prob_grad - mean) * SCALE
        mixes.append(jnp.concatenate([score_grad, weights], axis=0).astype(BF16))
    for (h, i), pair, mix in zip(units, pairs, mixes):
        column, tokens = slice(h * HD, (h + 1) * HD), slice(i * STRETCH, (i + 1) * STRETCH)
        keys = slice(i * NLEN, (i + 1) * NLEN)
        o = dot(mix, kv[h // 2, h % 2, keys, :])
        qg[tokens, column] = o[:STRETCH, :HD].astype(BF16)
        att[tokens, column] = o[STRETCH:, HD:].astype(BF16)
        kvg[h // 2, h % 2, keys, :] = dot_tn(mix, pair).astype(BF16)


def whole_kernel(
    slot_ref, gain_ref, pool_ref, wk_ref, wv_ref, up_ref, down_ref, q_ref, g_ref,
    att_ref, qg_ref, pg_ref, kw_ref, vw_ref,
    user, mid, out, rows, wall, up, down, q_all, g_all, att, qg, slope, inv, enc, enc_other,
    enct, kv, kvg, kvg_other, part, pg, mid2, out2, ya1, ya2, xa1, xa2, xb1, xb2, yb1, yb2,
    zbuf, fin, ssem, rsem, lsem,
):
    p = Place()
    z, c, x, y = p.z, p.c, p.x, p.y
    cp = Copies(ssem, rsem)

    def local(src, dst, index):
        return pltpu.make_async_copy(src, dst, lsem.at[index])

    def own_chunk(source):
        return local(source.at[x % 2, sub(y), :], wall.at[z, c, x, sub(y), :], 0)

    @pl.when(x < 2)
    def key_chunk():
        own_chunk(wk_ref).start()

    @pl.when(x >= 2)
    def value_chunk():
        own_chunk(wv_ref).start()

    own_slots = pl.ds(p.seq * CAP, CAP)
    own_pool = local(pool_ref.at[:, rows16(z), :], mid.at[own_slots], 1)
    own_pool.start()
    loads = [
        local(src, dst, 2 + n)
        for n, (src, dst) in enumerate(
            ((up_ref, up), (down_ref, down), (q_ref, q_all), (g_ref, g_all))
        )
    ]
    for load in loads:
        load.start()
    greet(
        [p.at_z(d) for d in range(1, NZ)] + [p.sibling()] + [p.at_dp(d) for d in range(1, NX * NX)]
    )

    own_chunk(wk_ref).wait()
    order = (4, 3, 5, 2, 6, 1, 7)

    def chunk(zz, xx, yy):
        return wall.at[zz, c, xx, sub(yy), :]

    wz = [cp.start(chunk(z, x, y), chunk(z, x, y), p.at_z(d)) for d in order]
    hop1 = {
        d: cp.start(pool_ref.at[:, rows16(p.zs(d)), :], mid.at[own_slots], p.at_z(d))
        for d in order
    }
    forward = [cp.start(pool_ref.at[:, rows16(z), :], mid.at[own_slots], p.sibling())]

    for copy in wz:
        copy.wait_recv()
    lo, hi = pl.ds(0, 4), pl.ds(4, 4)

    def ring(region, heads, places, at):
        src = region(heads, places(0))
        return [cp.start(src, src, at(1)), cp.start(src, src, at(-1))]

    def ring2(region, first, places, at, arrived):
        arrived[0].wait_recv()
        src = region(pl.ds(first, 2), places(-1))
        one = cp.start(src, src, at(1))
        arrived[1].wait_recv()
        src = region(pl.ds(first + 2, 2), places(1))
        return [one, cp.start(src, src, at(-1))]

    def row_x(heads, xx):
        return wall.at[heads, c, xx, sub(y), :]

    def row_y(heads, yy):
        return wall.at[heads, c, x, sub(yy), :]

    def wide_y(heads, yy):
        return wall.at[heads, c, :, sub(yy), :]

    def wide_x(heads, xx):
        return wall.at[heads, c, xx, :, :]

    sib = []

    def share(src):
        sib.append(cp.start(src, src, p.sibling()))

    def hand(distances):
        for d in distances:
            hop1[d].wait_recv()
            block = mid.at[pl.ds((p.zs(-d) * 2 + c) * CAP, CAP)]
            forward.append(cp.start(block, block, p.sibling()))

    a1 = ring(row_x, lo, p.xs, p.at_x)
    b1 = ring(row_y, hi, p.ys, p.at_y)
    a2 = ring2(row_x, 0, p.xs, p.at_x, a1)
    b2 = ring2(row_y, 4, p.ys, p.at_y, b1)
    for copy in a2:
        copy.wait_recv()
    a3 = ring(wide_y, lo, p.ys, p.at_y)
    for copy in b2:
        copy.wait_recv()
    b3 = ring(wide_x, hi, p.xs, p.at_x)
    share(wide_y(lo, y))
    share(wide_x(hi, x))
    own_pool.wait()
    hand((1, 7, 2, 6))

    def find_user(k, carry):
        slot = (p.zs(k // CAP) * 2 + c) * CAP + k % CAP
        found = jnp.int32(0)
        for stretch in range(SLOTS // 2):
            found = jnp.where(slot_ref[stretch] == slot, stretch + 1, found)
        user[k] = found
        return carry

    lax.fori_loop(0, NZ * CAP, find_user, 0)
    hand((3, 5, 4))
    for copy in forward:
        copy.wait_recv()
    hop2 = []
    for d in order + (0,):
        target = p.zs(d) * 2 + c
        for i in range(2):
            out[d, i] = mid[slot_ref[target * 2 + i]]
        dst = rows.at[:, rows16(z), :]
        if d == 0:
            own_rows = local(out.at[d], dst, 6)
            own_rows.start()
        else:
            hop2.append(cp.start(out.at[d], dst, p.at_z(d)))

    a4 = ring2(wide_y, 0, p.ys, p.at_y, a3)
    b4 = ring2(wide_x, 4, p.xs, p.at_x, b3)
    for d in (1, -1):
        share(wide_y(lo, p.ys(d)))
        share(wide_x(hi, p.xs(d)))
    for side in range(2):
        a4[side].wait_recv()
        share(wide_y(pl.ds(2 * side, 2), p.ys(2)))
        b4[side].wait_recv()
        share(wide_x(pl.ds(4 + 2 * side, 2), p.xs(2)))
    own_rows.wait()
    for copy in hop2:
        copy.wait_recv()

    for load in loads:
        load.wait()
    encoded = encode(rows, gain_ref, up, down, slope, inv)
    enc[...] = encoded
    enc_sent = cp.start(enc, enc_other, p.sibling())
    enct[:, :ROWS] = encoded.T
    for copy in sib:
        copy.wait_recv()

    def both(h):
        k = wall[h // 2, h % 2, pl.ds(0, 2)].reshape(DE, HD)
        v = wall[h // 2, h % 2, pl.ds(2, 2)].reshape(DE, HD)
        return jnp.concatenate([k, v], axis=1)

    kvg_sent = []
    for first in range(0, HEADS, GROUP):
        for h in range(first, first + GROUP):
            kv[h // 2, h % 2] = dot(enc[...], both(h)).astype(BF16)
        attention(first, GROUP, q_all, g_all, kv, kvg, att, qg)
        span = pl.ds(first // 2, GROUP // 2)
        kvg_sent.append(cp.start(kvg.at[span, 1 - c], kvg_other.at[span], p.sibling()))
    results = [local(att, att_ref, 7), local(qg, qg_ref, 8)]
    for result in results:
        result.start()
    total = jnp.zeros((ROWS, DE), F32)
    for h in range(HEADS):
        total = total + dot_nt(kvg[h // 2, h % 2], both(h))
    pg[...] = encode_back(
        total.astype(BF16), rows, gain_ref, up, down, slope, inv
    ).reshape(2, NLEN, DE)

    own_two = pl.ds(p.seq * 2 + 1, 2)
    own_mid = local(pg.at[:, rows16(z), :], mid2.at[own_two], 9)
    own_mid.start()
    back1 = {
        d: cp.start(pg.at[:, rows16(p.zs(d)), :], mid2.at[own_two], p.at_z(d)) for d in order
    }
    returns = [cp.start(pg.at[:, rows16(z), :], mid2.at[own_two], p.sibling())]
    mid2[0] = jnp.zeros((PIECE, DE), BF16)

    enc_sent.wait_recv()
    enct[:, ROWS:] = enc_other[...].T

    def weight_grad(h):
        grads = jnp.concatenate([kvg[h, c], kvg_other[h]], axis=0)
        block = dot(enct[...], grads).astype(BF16)
        for n in range(4):
            part[h, n] = block[(n % 2) * WROWS : (n % 2 + 1) * WROWS, (n // 2) * HD : (n // 2 + 1) * HD]

    def sum_y(first, count, yy):
        return part.at[pl.ds(first, count), :, sub(yy), :]

    def sum_x(first, count, xx):
        return part.at[pl.ds(first, count), xx, :, :]

    def narrow_x(first, count, xx):
        return part.at[pl.ds(first, count), xx, sub(y), :]

    def narrow_y(first, count, yy):
        return part.at[pl.ds(first, count), x, sub(yy), :]

    def far(region, first, places, at, land):
        return [
            cp.start(region(first, 2, places(2)), land.at[0], at(1)),
            cp.start(region(first + 2, 2, places(2)), land.at[1], at(-1)),
        ]

    def near(region, first, places, at, arrived, land1, land2):
        sent = []
        for side, d in ((0, 1), (1, -1)):
            arrived[side].wait_recv()
            block = region(first + 2 * side, 2, places(d))
            block[...] = (block[...].astype(F32) + land1[side].astype(F32)).astype(BF16)
            sent.append(cp.start(region(first, 4, places(d)), land2.at[side], at(d)))
        return sent

    def close(region, first, places, arrived, land2):
        for copy in arrived:
            copy.wait_recv()
        block = region(first, 4, places(0))
        block[...] = (
            block[...].astype(F32) + land2[0].astype(F32) + land2[1].astype(F32)
        ).astype(BF16)

    kvg_sent[0].wait_recv()
    for h in range(4):
        weight_grad(h)
    a1 = far(sum_y, 0, p.ys, p.at_y, ya1)
    kvg_sent[1].wait_recv()
    for h in range(4, NZ):
        weight_grad(h)
    b1 = far(sum_x, 4, p.xs, p.at_x, xb1)

    def give(distances):
        for d in distances:
            back1[d].wait_recv()
            block = mid2.at[pl.ds((p.zs(-d) * 2 + c) * 2 + 1, 2)]
            returns.append(cp.start(block, block, p.sibling()))

    give((1, 7, 2, 6))
    a2 = near(sum_y, 0, p.ys, p.at_y, a1, ya1, ya2)
    b2 = near(sum_x, 4, p.xs, p.at_x, b1, xb1, xb2)
    give((3, 5, 4))
    own_mid.wait()
    for copy in returns:
        copy.wait_recv()
    back2 = []
    for d in order + (0,):
        for j in range(CAP):
            out2[d, j] = mid2[user[d * CAP + j]]
        dst = pg_ref.at[:, rows16(z), :]
        if d == 0:
            own_back = local(out2.at[d], dst, 10)
            own_back.start()
        else:
            back2.append(cp.start(out2.at[d], dst, p.at_z(d)))

    close(sum_y, 0, p.ys, a2, ya2)
    a3 = far(narrow_x, 0, p.xs, p.at_x, xa1)
    close(sum_x, 4, p.xs, b2, xb2)
    b3 = far(narrow_y, 4, p.ys, p.at_y, yb1)
    a4 = near(narrow_x, 0, p.xs, p.at_x, a3, xa1, xa2)
    b4 = near(narrow_y, 4, p.ys, p.at_y, b3, yb1, yb2)
    close(narrow_x, 0, p.xs, a4, xa2)
    close(narrow_y, 4, p.ys, b4, yb2)
    zsum = [cp.start(part.at[p.zs(d), x, sub(y), :], zbuf.at[d], p.at_z(d)) for d in order]
    for copy in zsum:
        copy.wait_recv()
    total = part[z, x, sub(y), :].astype(F32)
    for d in range(1, NZ):
        total = total + zbuf[d].astype(F32)
    fin[x, y] = total.astype(BF16)
    last = [cp.start(fin.at[x, y], fin.at[x, y], p.at_dp(d)) for d in range(1, NX * NX)]
    for copy in last:
        copy.wait_recv()
    for xx in range(2):
        for yy in range(NX):
            span = slice(xx * WROWS + yy * WSUB, xx * WROWS + (yy + 1) * WSUB)
            kw_ref[span, :] = fin[xx, yy].astype(F32)
            vw_ref[span, :] = fin[xx + 2, yy].astype(F32)
    own_back.wait()
    for result in results:
        result.wait()
    for copy in back2:
        copy.wait_recv()
    cp.finish()


def whole(slots, gain, pool, wk, wv, up, down, queries, grads):
    anyspace = pl.BlockSpec(memory_space=pl.ANY)
    vmem = pl.BlockSpec(memory_space=pltpu.VMEM)
    width = HEADS * HD

    def scratch(*shape):
        return pltpu.VMEM(shape, BF16)

    return pl.pallas_call(
        whole_kernel,
        out_shape=(
            jax.ShapeDtypeStruct((TOKENS, width), BF16),
            jax.ShapeDtypeStruct((TOKENS, width), BF16),
            jax.ShapeDtypeStruct((CAP, NLEN, DE), BF16),
            jax.ShapeDtypeStruct((DE, HD), F32),
            jax.ShapeDtypeStruct((DE, HD), F32),
        ),
        in_specs=[pl.BlockSpec(memory_space=pltpu.SMEM), vmem] + [anyspace] * 7,
        out_specs=(anyspace, anyspace, anyspace, vmem, vmem),
        scratch_shapes=[
            pltpu.SMEM((NZ * CAP,), jnp.int32),
            scratch(SLOTS, PIECE, DE),
            scratch(NZ, 2, PIECE, DE),
            scratch(2, NLEN, DE),
            scratch(NZ, 2, 4, WROWS, HD),
            scratch(DE, FFE),
            scratch(FFE, DE),
            scratch(TOKENS, width),
            scratch(TOKENS, width),
            scratch(TOKENS, width),
            scratch(TOKENS, width),
            pltpu.VMEM((ROWS, FFE), F32),
            pltpu.VMEM((ROWS, 1), F32),
            scratch(ROWS, DE),
            scratch(ROWS, DE),
            scratch(DE, 2 * ROWS),
            scratch(NZ, 2, ROWS, 2 * HD),
            scratch(NZ, 2, ROWS, 2 * HD),
            scratch(NZ, ROWS, 2 * HD),
            scratch(NZ, 4, WROWS, HD),
            scratch(2, NLEN, DE),
            scratch(1 + SLOTS // 2, PIECE, DE),
            scratch(NZ, CAP, PIECE, DE),
            scratch(2, 2, 4, WSUB, HD),
            scratch(2, 4, 4, WSUB, HD),
            scratch(2, 2, WSUB, HD),
            scratch(2, 4, WSUB, HD),
            scratch(2, 2, WROWS, HD),
            scratch(2, 4, WROWS, HD),
            scratch(2, 2, WSUB, HD),
            scratch(2, 4, WSUB, HD),
            scratch(NZ, WSUB, HD),
            scratch(NX, NX, WSUB, HD),
            pltpu.SemaphoreType.DMA((COPIES,)),
            pltpu.SemaphoreType.DMA((COPIES,)),
            pltpu.SemaphoreType.DMA((11,)),
        ],
        compiler_params=pltpu.CompilerParams(
            collective_id=0, has_side_effects=True, vmem_limit_bytes=56 * 1024 * 1024
        ),
        name="whole",
    )(slots, gain, pool, wk, wv, up, down, queries, grads)


def on_device(queries, attended_grad, pool, stretch_slot, gain, up, down, key_w, value_w):
    attended, query_grad, pool_grad, key_grad, value_grad = whole(
        stretch_slot[0],
        gain.reshape(1, DE),
        pool[0],
        key_w.reshape(2, WROWS, HD),
        value_w.reshape(2, WROWS, HD),
        up,
        down,
        queries[0],
        attended_grad[0],
    )
    return attended[None], query_grad[None], pool_grad[None], key_grad, value_grad


def solution(mesh):
    return jax.shard_map(
        on_device,
        mesh=mesh,
        in_specs=(
            P("dp", "seq", None),
            P("dp", "seq", None),
            P("dp", "seq", None, None),
            P("dp", None),
            P(),
            P(),
            P(),
            P(None, "seq"),
            P(None, "seq"),
        ),
        out_specs=(
            P("dp", "seq", None),
            P("dp", "seq", None),
            P("dp", "seq", None, None),
            P(None, "seq"),
            P(None, "seq"),
        ),
        check_vma=False,
    )
```

time: 165 us -> 125 us (0.76)
  Pallas kernels: 146 us -> 116 us
  local copies, waits for them, and re-layouts: 16.9 us -> 8.82 us
    pallas_call x3 -> x1, Pallas kernels: 146 us -> 116 us  [whole(): pl.pallas_call(whole_kernel, out_shape=(jax.ShapeDtypeStruct((TOKENS, wid...]
    unnamed x23 -> x9, local copies, waits for them, and re-layouts: 16.2 us -> 7.56 us
where the time goes in v2:
time: 125 us
  Pallas kernels  116 us (93%)
  local copies, waits for them, and re-layouts  8.82 us (7%)
    pallas_call x1, Pallas kernels, whole(): pl.pallas_call(whole_kernel, out_shape=(jax.ShapeDtypeStruct((TOKENS, wid...  116 us
    unnamed x9, local copies, waits for them, and re-layouts  7.56 us

profile of v2, /device:TPU:1, one launch (start us, length us, event | category | flops | bytes accessed | tf_op | source)
XLA Modules:
  0.0 125.2 jit_solution(2717818918337881311)
XLA Ops:
  0.6 1.3 %reshape.19.gain_ref = f32[1,896]{1,0:T(1,128)} reshape(f32[896]{0:T(1024)} %param.13) | data formatting | bytes 7168 | tf_op jit(solution)/shard_map/reshape | solution.py:545
  1.9 115.7 %whole.1 = (bf16[128,2048]{1,0:T(8,128)(2,1)}, bf16[128,2048]{1,0:T(8,128)(2,1)}, bf16[4,128,896]{2,1,0:T(8,128)(2,1)}, f32[896,128]{1,0:T(8,128)}, f32[896,128]{1,0:T(8,128)}) custom-call(s32[32]{0:T(128)} %bitcast.17, f32[1,896]{1,0:T(1,128)} %reshape.19.gain_ref, bf16[4,128,896]{2,1,0:T(8,128)(2,1)} %bitcast.10, bf16[2,448,128]{2,1,0:T(8,128)(2,1)} %bitcast.15, ...), custom_call_target="tpu_custom_call" | custom-call | tf_op jit(solution)/shard_map/whole/pallas_call | solution.py:486
  117.6 0.0 copy-start.1
  117.6 0.0 copy-start
  117.6 2.0 %copy.19 = bf16[1,128,2048]{2,1,0:T(8,128)(2,1)} copy(bf16[1,128,2048]{2,1,0:T(8,128)(2,1)} %bitcast.14) | data formatting | bytes 1048576
  119.6 1.9 %copy.20 = bf16[1,128,2048]{2,1,0:T(8,128)(2,1)} copy(bf16[1,128,2048]{2,1,0:T(8,128)(2,1)} %bitcast.13) | data formatting | bytes 1048576
  121.5 2.2 %copy.21 = bf16[1,4,128,896]{3,2,1,0:T(8,128)(2,1)} copy(bf16[1,4,128,896]{3,2,1,0:T(8,128)(2,1)} %bitcast.9) | data formatting | bytes 1835008
  123.7 0.0 copy-done.1
  123.7 0.8 copy.22
  124.4 0.0 copy-done
  124.4 0.8 copy.23
Async XLA Ops:
  117.6 6.0 %copy-start.1 = (f32[896,128]{1,0:T(8,128)S(1)}, f32[896,128]{1,0:T(8,128)}, u32[]{:S(2)}) copy-start(f32[896,128]{1,0:T(8,128)} %get-tuple-element.23) | copy-start | bytes 1376260
  117.6 6.8 %copy-start = (f32[896,128]{1,0:T(8,128)S(1)}, f32[896,128]{1,0:T(8,128)}, u32[]{:S(2)}) copy-start(f32[896,128]{1,0:T(8,128)} %get-tuple-element.24) | copy-start | bytes 1376260

commit v3 on v2

--- a/solution.py
+++ b/solution.py
@@ -103,7 +103,8 @@
     return pl.ds(pl.multiple_of(index * WSUB, 16), WSUB)
 
 
-COPIES = 136
+COPIES = 192
+HALVES = (slice(0, 512), slice(512, DE))
 GROUP = 8
 TILE = 256
 ROWS = 2 * NLEN
@@ -125,7 +126,7 @@
     rows = rows_ref[...].reshape(ROWS, DE).astype(F32)
     inverse = lax.rsqrt(jnp.mean(rows * rows, axis=-1, keepdims=True) + EPS)
     inv[...] = inverse
-    normed = (rows * inverse * gain_ref[...]).astype(BF16)
+    normed = (rows * inverse * gain_ref[...].reshape(1, DE)).astype(BF16)
     root = math.sqrt(2.0 / math.pi)
     before = dot(normed, up[...])
     square = before * before
@@ -140,7 +141,7 @@
     normed_grad = dot_nt(before_grad, up[...])
     rows = rows_ref[...].reshape(ROWS, DE).astype(F32)
     inverse = inv[...]
-    scaled = gain_ref[...] * normed_grad
+    scaled = gain_ref[...].reshape(1, DE) * normed_grad
     result = (
         encoded_grad.astype(F32)
         + inverse * scaled
@@ -184,9 +185,10 @@
 
 def whole_kernel(
     slot_ref, gain_ref, pool_ref, wk_ref, wv_ref, up_ref, down_ref, q_ref, g_ref,
-    att_ref, qg_ref, pg_ref, kw_ref, vw_ref,
-    user, mid, out, rows, wall, up, down, q_all, g_all, att, qg, slope, inv, enc, enc_other,
-    enct, kv, kvg, kvg_other, part, pg, mid2, out2, ya1, ya2, xa1, xa2, xb1, xb2, yb1, yb2,
+    att_ref, qg_ref, pg_ref, fin_ref,
+    user, mid_a, mid_b, out_a, out_b, rows, wall, up, down, q_all, g_all, att, qg, slope, inv, enc, enc_other,
+    enct, kv, kvg, kvg_other, part, pg,
+    mid2_a, mid2_b, out2_a, out2_b, ya1, ya2, xa1, xa2, xb1, xb2, yb1, yb2,
     zbuf, fin, ssem, rsem, lsem,
 ):
     p = Place()
@@ -208,8 +210,14 @@
         own_chunk(wv_ref).start()
 
     own_slots = pl.ds(p.seq * CAP, CAP)
-    own_pool = local(pool_ref.at[:, rows16(z), :], mid.at[own_slots], 1)
-    own_pool.start()
+    mid, out = (mid_a, mid_b), (out_a, out_b)
+    mid2, out2 = (mid2_a, mid2_b), (out2_a, out2_b)
+    own_pool = [
+        local(pool_ref.at[:, rows16(z), part_of], mid[n].at[own_slots], (1, 11)[n])
+        for n, part_of in enumerate(HALVES)
+    ]
+    for copy in own_pool:
+        copy.start()
     loads = [
         local(src, dst, 2 + n)
         for n, (src, dst) in enumerate(
@@ -229,11 +237,19 @@
         return wall.at[zz, c, xx, sub(yy), :]
 
     wz = [cp.start(chunk(z, x, y), chunk(z, x, y), p.at_z(d)) for d in order]
-    hop1 = {
-        d: cp.start(pool_ref.at[:, rows16(p.zs(d)), :], mid.at[own_slots], p.at_z(d))
-        for d in order
-    }
-    forward = [cp.start(pool_ref.at[:, rows16(z), :], mid.at[own_slots], p.sibling())]
+    hop1, forward = [], []
+    for n, part_of in enumerate(HALVES):
+        hop1.append(
+            {
+                d: cp.start(
+                    pool_ref.at[:, rows16(p.zs(d)), part_of], mid[n].at[own_slots], p.at_z(d)
+                )
+                for d in order
+            }
+        )
+        forward.append(
+            [cp.start(pool_ref.at[:, rows16(z), part_of], mid[n].at[own_slots], p.sibling())]
+        )
 
     for copy in wz:
         copy.wait_recv()
@@ -268,11 +284,29 @@
     def share(src):
         sib.append(cp.start(src, src, p.sibling()))
 
-    def hand(distances):
-        for d in distances:
-            hop1[d].wait_recv()
-            block = mid.at[pl.ds((p.zs(-d) * 2 + c) * CAP, CAP)]
-            forward.append(cp.start(block, block, p.sibling()))
+    hop2 = []
+    own_rows = [
+        local(out[n].at[0], rows.at[:, rows16(z), part_of], (6, 12)[n])
+        for n, part_of in enumerate(HALVES)
+    ]
+
+    def pool_step(n):
+        for d in (1, 7, 2, 6, 3, 5, 4):
+            hop1[n][d].wait_recv()
+            block = mid[n].at[pl.ds((p.zs(-d) * 2 + c) * CAP, CAP)]
+            forward[n].append(cp.start(block, block, p.sibling()))
+        own_pool[n].wait()
+        for copy in forward[n]:
+            copy.wait_recv()
+        for d in order + (0,):
+            target = p.zs(d) * 2 + c
+            for i in range(2):
+                out[n][d, i] = mid[n][slot_ref[target * 2 + i]]
+            if d == 0:
+                own_rows[n].start()
+            else:
+                dst = rows.at[:, rows16(z), HALVES[n]]
+                hop2.append(cp.start(out[n].at[d], dst, p.at_z(d)))
 
     a1 = ring(row_x, lo, p.xs, p.at_x)
     b1 = ring(row_y, hi, p.ys, p.at_y)
@@ -286,9 +320,6 @@
     b3 = ring(wide_x, hi, p.xs, p.at_x)
     share(wide_y(lo, y))
     share(wide_x(hi, x))
-    own_pool.wait()
-    hand((1, 7, 2, 6))
-
     def find_user(k, carry):
         slot = (p.zs(k // CAP) * 2 + c) * CAP + k % CAP
         found = jnp.int32(0)
@@ -298,32 +329,20 @@
         return carry
 
     lax.fori_loop(0, NZ * CAP, find_user, 0)
-    hand((3, 5, 4))
-    for copy in forward:
-        copy.wait_recv()
-    hop2 = []
-    for d in order + (0,):
-        target = p.zs(d) * 2 + c
-        for i in range(2):
-            out[d, i] = mid[slot_ref[target * 2 + i]]
-        dst = rows.at[:, rows16(z), :]
-        if d == 0:
-            own_rows = local(out.at[d], dst, 6)
-            own_rows.start()
-        else:
-            hop2.append(cp.start(out.at[d], dst, p.at_z(d)))
-
+    pool_step(0)
     a4 = ring2(wide_y, 0, p.ys, p.at_y, a3)
     b4 = ring2(wide_x, 4, p.xs, p.at_x, b3)
     for d in (1, -1):
         share(wide_y(lo, p.ys(d)))
         share(wide_x(hi, p.xs(d)))
+    pool_step(1)
     for side in range(2):
         a4[side].wait_recv()
         share(wide_y(pl.ds(2 * side, 2), p.ys(2)))
         b4[side].wait_recv()
         share(wide_x(pl.ds(4 + 2 * side, 2), p.xs(2)))
-    own_rows.wait()
+    for copy in own_rows:
+        copy.wait()
     for copy in hop2:
         copy.wait_recv()
 
@@ -351,22 +370,6 @@
     results = [local(att, att_ref, 7), local(qg, qg_ref, 8)]
     for result in results:
         result.start()
-    total = jnp.zeros((ROWS, DE), F32)
-    for h in range(HEADS):
-        total = total + dot_nt(kvg[h // 2, h % 2], both(h))
-    pg[...] = encode_back(
-        total.astype(BF16), rows, gain_ref, up, down, slope, inv
-    ).reshape(2, NLEN, DE)
-
-    own_two = pl.ds(p.seq * 2 + 1, 2)
-    own_mid = local(pg.at[:, rows16(z), :], mid2.at[own_two], 9)
-    own_mid.start()
-    back1 = {
-        d: cp.start(pg.at[:, rows16(p.zs(d)), :], mid2.at[own_two], p.at_z(d)) for d in order
-    }
-    returns = [cp.start(pg.at[:, rows16(z), :], mid2.at[own_two], p.sibling())]
-    mid2[0] = jnp.zeros((PIECE, DE), BF16)
-
     enc_sent.wait_recv()
     enct[:, ROWS:] = enc_other[...].T
 
@@ -420,30 +423,51 @@
         weight_grad(h)
     b1 = far(sum_x, 4, p.xs, p.at_x, xb1)
 
-    def give(distances):
-        for d in distances:
-            back1[d].wait_recv()
-            block = mid2.at[pl.ds((p.zs(-d) * 2 + c) * 2 + 1, 2)]
-            returns.append(cp.start(block, block, p.sibling()))
-
-    give((1, 7, 2, 6))
+    total = jnp.zeros((ROWS, DE), F32)
+    for h in range(HEADS):
+        total = total + dot_nt(kvg[h // 2, h % 2], both(h))
+    pg[...] = encode_back(
+        total.astype(BF16), rows, gain_ref, up, down, slope, inv
+    ).reshape(2, NLEN, DE)
+
+    own_two = pl.ds(p.seq * 2 + 1, 2)
+    own_mid, back1, returns, back2, own_back = [], [], [], [], []
+    for n, part_of in enumerate(HALVES):
+        own_mid.append(local(pg.at[:, rows16(z), part_of], mid2[n].at[own_two], (9, 13)[n]))
+        own_mid[n].start()
+        back1.append(
+            {
+                d: cp.start(pg.at[:, rows16(p.zs(d)), part_of], mid2[n].at[own_two], p.at_z(d))
+                for d in order
+            }
+        )
+        returns.append(
+            [cp.start(pg.at[:, rows16(z), part_of], mid2[n].at[own_two], p.sibling())]
+        )
+        mid2[n][0] = jnp.zeros(mid2[n].shape[1:], BF16)
+        own_back.append(local(out2[n].at[0], pg_ref.at[:, rows16(z), part_of], (10, 14)[n]))
+
+    def back_step(n):
+        for d in (1, 7, 2, 6, 3, 5, 4):
+            back1[n][d].wait_recv()
+            block = mid2[n].at[pl.ds((p.zs(-d) * 2 + c) * 2 + 1, 2)]
+            returns[n].append(cp.start(block, block, p.sibling()))
+        own_mid[n].wait()
+        for copy in returns[n]:
+            copy.wait_recv()
+        for d in order + (0,):
+            for j in range(CAP):
+                out2[n][d, j] = mid2[n][user[d * CAP + j]]
+            if d == 0:
+                own_back[n].start()
+            else:
+                dst = pg_ref.at[:, rows16(z), HALVES[n]]
+                back2.append(cp.start(out2[n].at[d], dst, p.at_z(d)))
+
     a2 = near(sum_y, 0, p.ys, p.at_y, a1, ya1, ya2)
     b2 = near(sum_x, 4, p.xs, p.at_x, b1, xb1, xb2)
-    give((3, 5, 4))
-    own_mid.wait()
-    for copy in returns:
-        copy.wait_recv()
-    back2 = []
-    for d in order + (0,):
-        for j in range(CAP):
-            out2[d, j] = mid2[user[d * CAP + j]]
-        dst = pg_ref.at[:, rows16(z), :]
-        if d == 0:
-            own_back = local(out2.at[d], dst, 10)
-            own_back.start()
-        else:
-            back2.append(cp.start(out2.at[d], dst, p.at_z(d)))
-
+    back_step(0)
+    back_step(1)
     close(sum_y, 0, p.ys, a2, ya2)
     a3 = far(narrow_x, 0, p.xs, p.at_x, xa1)
     close(sum_x, 4, p.xs, b2, xb2)
@@ -462,16 +486,15 @@
     last = [cp.start(fin.at[x, y], fin.at[x, y], p.at_dp(d)) for d in range(1, NX * NX)]
     for copy in last:
         copy.wait_recv()
-    for xx in range(2):
-        for yy in range(NX):
-            span = slice(xx * WROWS + yy * WSUB, xx * WROWS + (yy + 1) * WSUB)
-            kw_ref[span, :] = fin[xx, yy].astype(F32)
-            vw_ref[span, :] = fin[xx + 2, yy].astype(F32)
-    own_back.wait()
+    written = local(fin, fin_ref, 15)
+    written.start()
+    for copy in own_back:
+        copy.wait()
     for result in results:
         result.wait()
     for copy in back2:
         copy.wait_recv()
+    written.wait()
     cp.finish()
 
 
@@ -489,15 +512,16 @@
             jax.ShapeDtypeStruct((TOKENS, width), BF16),
             jax.ShapeDtypeStruct((TOKENS, width), BF16),
             jax.ShapeDtypeStruct((CAP, NLEN, DE), BF16),
-            jax.ShapeDtypeStruct((DE, HD), F32),
-            jax.ShapeDtypeStruct((DE, HD), F32),
+            jax.ShapeDtypeStruct((NX, NX, WSUB, HD), BF16),
         ),
         in_specs=[pl.BlockSpec(memory_space=pltpu.SMEM), vmem] + [anyspace] * 7,
-        out_specs=(anyspace, anyspace, anyspace, vmem, vmem),
+        out_specs=(anyspace,) * 4,
         scratch_shapes=[
             pltpu.SMEM((NZ * CAP,), jnp.int32),
-            scratch(SLOTS, PIECE, DE),
-            scratch(NZ, 2, PIECE, DE),
+            scratch(SLOTS, PIECE, 512),
+            scratch(SLOTS, PIECE, DE - 512),
+            scratch(NZ, 2, PIECE, 512),
+            scratch(NZ, 2, PIECE, DE - 512),
             scratch(2, NLEN, DE),
             scratch(NZ, 2, 4, WROWS, HD),
             scratch(DE, FFE),
@@ -516,8 +540,10 @@
             scratch(NZ, ROWS, 2 * HD),
             scratch(NZ, 4, WROWS, HD),
             scratch(2, NLEN, DE),
-            scratch(1 + SLOTS // 2, PIECE, DE),
-            scratch(NZ, CAP, PIECE, DE),
+            scratch(1 + SLOTS // 2, PIECE, 512),
+            scratch(1 + SLOTS // 2, PIECE, DE - 512),
+            scratch(NZ, CAP, PIECE, 512),
+            scratch(NZ, CAP, PIECE, DE - 512),
             scratch(2, 2, 4, WSUB, HD),
             scratch(2, 4, 4, WSUB, HD),
             scratch(2, 2, WSUB, HD),
@@ -530,7 +556,7 @@
             scratch(NX, NX, WSUB, HD),
             pltpu.SemaphoreType.DMA((COPIES,)),
             pltpu.SemaphoreType.DMA((COPIES,)),
-            pltpu.SemaphoreType.DMA((11,)),
+            pltpu.SemaphoreType.DMA((16,)),
         ],
         compiler_params=pltpu.CompilerParams(
             collective_id=0, has_side_effects=True, vmem_limit_bytes=56 * 1024 * 1024
@@ -539,17 +565,60 @@
     )(slots, gain, pool, wk, wv, up, down, queries, grads)
 
 
+def place_kernel(att, qg, pg, fin, att_out, qg_out, pg_out, kw_out, vw_out, wide, key, value, sems):
+    load = pltpu.make_async_copy(fin, wide, sems.at[0])
+    load.start()
+    copies = []
+    for src, dst, cut in ((pg, pg_out, 4), (att, att_out, 2), (qg, qg_out, 2)):
+        size = src.shape[0] // cut
+        for n in range(cut):
+            span = pl.ds(n * size, size)
+            copies.append(
+                pltpu.make_async_copy(src.at[span], dst.at[span], sems.at[1 + len(copies)])
+            )
+            copies[-1].start()
+    load.wait()
+    for n, (held, dst) in enumerate(((key, kw_out), (value, vw_out))):
+        held[...] = wide[2 * n : 2 * n + 2].reshape(DE, HD).astype(F32)
+        copies.append(pltpu.make_async_copy(held, dst, sems.at[1 + len(copies)]))
+        copies[-1].start()
+    for copy in copies:
+        copy.wait()
+
+
+def place(att, qg, pg, fin):
+    anyspace = pl.BlockSpec(memory_space=pl.ANY)
+    shapes = [jax.ShapeDtypeStruct(a.shape, a.dtype) for a in (att, qg, pg)]
+    grad = jax.ShapeDtypeStruct((DE, HD), F32)
+    return pl.pallas_call(
+        place_kernel,
+        out_shape=(*shapes, grad, grad),
+        in_specs=[anyspace] * 4,
+        out_specs=(anyspace,) * 5,
+        scratch_shapes=[
+            pltpu.VMEM((NX, NX, WSUB, HD), BF16),
+            pltpu.VMEM((DE, HD), F32),
+            pltpu.VMEM((DE, HD), F32),
+            pltpu.SemaphoreType.DMA((11,)),
+        ],
+        compiler_params=pltpu.CompilerParams(vmem_limit_bytes=56 * 1024 * 1024),
+        name="place",
+    )(att, qg, pg, fin)
+
+
 def on_device(queries, attended_grad, pool, stretch_slot, gain, up, down, key_w, value_w):
-    attended, query_grad, pool_grad, key_grad, value_grad = whole(
-        stretch_slot[0],
-        gain.reshape(1, DE),
-        pool[0],
-        key_w.reshape(2, WROWS, HD),
-        value_w.reshape(2, WROWS, HD),
-        up,
-        down,
-        queries[0],
-        attended_grad[0],
+    attended, query_grad, pool_grad, key_grad, value_grad = place(
+        *whole(
+            stretch_slot[0],
+            gain,
+            pool[0],
+            key_w.reshape(2, WROWS, HD),
+            value_w.reshape(2, WROWS, HD),
+            up,
+            down,
+            queries[0],
+            attended_grad[0],
+        )
     )
     return attended[None], query_grad[None], pool_grad[None], key_grad, value_grad
 

time: 125 us -> 177 us (1.42)
  Pallas kernels: 116 us -> 176 us
  local copies, waits for them, and re-layouts: 8.82 us -> 0 us
    pallas_call x0 -> x1, Pallas kernels: none -> 60.8 us  [place(): pl.pallas_call(place_kernel, out_shape=(*shapes, grad, grad), in_specs=[a...]
    unnamed x9 -> x0, local copies, waits for them, and re-layouts: 7.56 us -> none
where the time goes in v3:
time: 177 us; the launch traced here: 176 us
  Pallas kernels  176 us (99%)
    pallas_call x1, Pallas kernels, whole(): pl.pallas_call(whole_kernel, out_shape=(jax.ShapeDtypeStruct((TOKENS, wid...  115 us
    pallas_call x1, Pallas kernels, place(): pl.pallas_call(place_kernel, out_shape=(*shapes, grad, grad), in_specs=[a...  60.8 us

profile of v3, /device:TPU:1, one launch (start us, length us, event | category | flops | bytes accessed | tf_op | source)
XLA Modules:
  0.0 176.5 jit_solution(8977003614547885946)
XLA Ops:
  0.6 114.9 %whole.1 = (bf16[128,2048]{1,0:T(8,128)(2,1)}, bf16[128,2048]{1,0:T(8,128)(2,1)}, bf16[4,128,896]{2,1,0:T(8,128)(2,1)}, bf16[4,4,112,128]{3,2,1,0:T(8,128)(2,1)}) custom-call(s32[32]{0:T(128)} %bitcast.14, f32[896]{0:T(1024)} %gain_ref.1, bf16[4,128,896]{2,1,0:T(8,128)(2,1)} %bitcast.9, bf16[2,448,128]{2,1,0:T(8,128)(2,1)} %bitcast.12, ...), custom_call_target="tpu_custom_call" | custom-call | tf_op jit(solution)/shard_map/whole/pallas_call | solution.py:509
  115.6 60.8 %place.1 = (bf16[128,2048]{1,0:T(8,128)(2,1)}, bf16[128,2048]{1,0:T(8,128)(2,1)}, bf16[4,128,896]{2,1,0:T(8,128)(2,1)}, f32[896,128]{1,0:T(8,128)}, f32[896,128]{1,0:T(8,128)}) custom-call(bf16[128,2048]{1,0:T(8,128)(2,1)} %get-tuple-element.14.att, bf16[128,2048]{1,0:T(8,128)(2,1)} %get-tuple-element.15.qg, bf16[4,128,896]{2,1,0:T(8,128)(2,1)} %get-tuple-element.16.pg, ...), custom_call_target="tpu_custom_call" | custom-call | tf_op jit(solution)/shard_map/place/pallas_call | solution.py:593

commit v4 on v3

--- a/solution.py
+++ b/solution.py
@@ -335,12 +335,12 @@
     for d in (1, -1):
         share(wide_y(lo, p.ys(d)))
         share(wide_x(hi, p.xs(d)))
-    pool_step(1)
     for side in range(2):
         a4[side].wait_recv()
         share(wide_y(pl.ds(2 * side, 2), p.ys(2)))
         b4[side].wait_recv()
         share(wide_x(pl.ds(4 + 2 * side, 2), p.xs(2)))
+    pool_step(1)
     for copy in own_rows:
         copy.wait()
     for copy in hop2:
@@ -458,6 +458,9 @@
         for d in order + (0,):
             for j in range(CAP):
                 out2[n][d, j] = mid2[n][user[d * CAP + j]]
+
+    def back_send(n):
+        for d in order + (0,):
             if d == 0:
                 own_back[n].start()
             else:
@@ -467,6 +470,7 @@
     a2 = near(sum_y, 0, p.ys, p.at_y, a1, ya1, ya2)
     b2 = near(sum_x, 4, p.xs, p.at_x, b1, xb1, xb2)
     back_step(0)
+    back_send(0)
     back_step(1)
     close(sum_y, 0, p.ys, a2, ya2)
     a3 = far(narrow_x, 0, p.xs, p.at_x, xa1)
@@ -477,6 +481,7 @@
     close(narrow_x, 0, p.xs, a4, xa2)
     close(narrow_y, 4, p.ys, b4, yb2)
     zsum = [cp.start(part.at[p.zs(d), x, sub(y), :], zbuf.at[d], p.at_z(d)) for d in order]
+    back_send(1)
     for copy in zsum:
         copy.wait_recv()
     total = part[z, x, sub(y), :].astype(F32)
@@ -565,25 +570,38 @@
     )(slots, gain, pool, wk, wv, up, down, queries, grads)
 
 
-def place_kernel(att, qg, pg, fin, att_out, qg_out, pg_out, kw_out, vw_out, wide, key, value, sems):
-    load = pltpu.make_async_copy(fin, wide, sems.at[0])
-    load.start()
-    copies = []
-    for src, dst, cut in ((pg, pg_out, 4), (att, att_out, 2), (qg, qg_out, 2)):
+def place_kernel(
+    att, qg, pg, fin, att_out, qg_out, pg_out, kw_out, vw_out,
+    wide, key, value, att_held, qg_held, pg_held, sems,
+):
+    loads, stores = [], []
+
+    def move(src, held, dst):
+        loads.append(pltpu.make_async_copy(src, held, sems.at[len(loads)]))
+        stores.append(pltpu.make_async_copy(held, dst, sems.at[16 + len(stores)]))
+        loads[-1].start()
+
+    wide_load = pltpu.make_async_copy(fin, wide, sems.at[15])
+    wide_load.start()
+    for src, held, dst, cut in (
+        (pg, pg_held, pg_out, 4),
+        (att, att_held, att_out, 2),
+        (qg, qg_held, qg_out, 2),
+    ):
         size = src.shape[0] // cut
         for n in range(cut):
             span = pl.ds(n * size, size)
-            copies.append(
-                pltpu.make_async_copy(src.at[span], dst.at[span], sems.at[1 + len(copies)])
-            )
-            copies[-1].start()
-    load.wait()
+            move(src.at[span], held.at[span], dst.at[span])
+    wide_load.wait()
     for n, (held, dst) in enumerate(((key, kw_out), (value, vw_out))):
         held[...] = wide[2 * n : 2 * n + 2].reshape(DE, HD).astype(F32)
-        copies.append(pltpu.make_async_copy(held, dst, sems.at[1 + len(copies)]))
-        copies[-1].start()
-    for copy in copies:
-        copy.wait()
+        stores.append(pltpu.make_async_copy(held, dst, sems.at[16 + len(stores)]))
+        stores[-1].start()
+    for load, store in zip(loads, stores):
+        load.wait()
+        store.start()
+    for store in stores:
+        store.wait()
 
 
 def place(att, qg, pg, fin):
@@ -599,7 +617,10 @@
             pltpu.VMEM((NX, NX, WSUB, HD), BF16),
             pltpu.VMEM((DE, HD), F32),
             pltpu.VMEM((DE, HD), F32),
-            pltpu.SemaphoreType.DMA((11,)),
+            pltpu.VMEM(att.shape, BF16),
+            pltpu.VMEM(qg.shape, BF16),
+            pltpu.VMEM(pg.shape, BF16),
+            pltpu.SemaphoreType.DMA((32,)),
         ],
         compiler_params=pltpu.CompilerParams(vmem_limit_bytes=56 * 1024 * 1024),
         name="place",

time: 177 us -> 115 us (0.65)
  Pallas kernels: 176 us -> 114 us
    pallas_call x1, Pallas kernels: 60.8 us -> 2.9 us  [place(): pl.pallas_call(place_kernel, out_shape=(*shapes, grad, grad), in_specs=[a...]
    pallas_call x1, Pallas kernels: 115 us -> 111 us  [whole(): pl.pallas_call(whole_kernel, out_shape=(jax.ShapeDtypeStruct((TOKENS, wid...]
where the time goes in v4:
time: 115 us
  Pallas kernels  114 us (99%)
    pallas_call x1, Pallas kernels, whole(): pl.pallas_call(whole_kernel, out_shape=(jax.ShapeDtypeStruct((TOKENS, wid...  111 us
    pallas_call x1, Pallas kernels, place(): pl.pallas_call(place_kernel, out_shape=(*shapes, grad, grad), in_specs=[a...  2.9 us

profile of v4, /device:TPU:1, one launch (start us, length us, event | category | flops | bytes accessed | tf_op | source)
XLA Modules:
  0.0 114.7 jit_solution(6451248133338179417)
XLA Ops:
  0.6 111.0 %whole.1 = (bf16[128,2048]{1,0:T(8,128)(2,1)}, bf16[128,2048]{1,0:T(8,128)(2,1)}, bf16[4,128,896]{2,1,0:T(8,128)(2,1)}, bf16[4,4,112,128]{3,2,1,0:T(8,128)(2,1)}) custom-call(s32[32]{0:T(128)} %bitcast.14, f32[896]{0:T(1024)} %gain_ref.1, bf16[4,128,896]{2,1,0:T(8,128)(2,1)} %bitcast.9, bf16[2,448,128]{2,1,0:T(8,128)(2,1)} %bitcast.12, ...), custom_call_target="tpu_custom_call" | custom-call | tf_op jit(solution)/shard_map/whole/pallas_call | solution.py:514
  111.7 2.9 %place.1 = (bf16[128,2048]{1,0:T(8,128)(2,1)}, bf16[128,2048]{1,0:T(8,128)(2,1)}, bf16[4,128,896]{2,1,0:T(8,128)(2,1)}, f32[896,128]{1,0:T(8,128)}, f32[896,128]{1,0:T(8,128)}) custom-call(bf16[128,2048]{1,0:T(8,128)(2,1)} %get-tuple-element.14.att, bf16[128,2048]{1,0:T(8,128)(2,1)} %get-tuple-element.15.qg, bf16[4,128,896]{2,1,0:T(8,128)(2,1)} %get-tuple-element.16.pg, ...), custom_call_target="tpu_custom_call" | custom-call | tf_op jit(solution)/shard_map/place/pallas_call | solution.py:611

commit v5 on v4

--- a/solution.py
+++ b/solution.py
@@ -104,7 +104,8 @@
 
 
 COPIES = 192
-HALVES = (slice(0, 512), slice(512, DE))
+SPLIT = 640
+HALVES = (slice(0, SPLIT), slice(SPLIT, DE))
 GROUP = 8
 TILE = 256
 ROWS = 2 * NLEN
@@ -235,6 +236,11 @@
 
     def chunk(zz, xx, yy):
         return wall.at[zz, c, xx, sub(yy), :]
+
+    pieces = ((0, 64), (64, WSUB - 64))
+
+    def rows_of(piece):
+        return pl.ds(pl.multiple_of(y * WSUB + piece[0], 16), piece[1])
 
     wz = [cp.start(chunk(z, x, y), chunk(z, x, y), p.at_z(d)) for d in order]
     hop1, forward = [], []
@@ -335,12 +341,12 @@
     for d in (1, -1):
         share(wide_y(lo, p.ys(d)))
         share(wide_x(hi, p.xs(d)))
+    pool_step(1)
     for side in range(2):
         a4[side].wait_recv()
         share(wide_y(pl.ds(2 * side, 2), p.ys(2)))
         b4[side].wait_recv()
         share(wide_x(pl.ds(4 + 2 * side, 2), p.xs(2)))
-    pool_step(1)
     for copy in own_rows:
         copy.wait()
     for copy in hop2:
@@ -432,7 +438,9 @@
 
     own_two = pl.ds(p.seq * 2 + 1, 2)
     own_mid, back1, returns, back2, own_back = [], [], [], [], []
-    for n, part_of in enumerate(HALVES):
+
+    def back_start(n):
+        part_of = HALVES[n]
         own_mid.append(local(pg.at[:, rows16(z), part_of], mid2[n].at[own_two], (9, 13)[n]))
         own_mid[n].start()
         back1.append(
@@ -446,6 +454,8 @@
         )
         mid2[n][0] = jnp.zeros(mid2[n].shape[1:], BF16)
         own_back.append(local(out2[n].at[0], pg_ref.at[:, rows16(z), part_of], (10, 14)[n]))
+
+    back_start(0)
 
     def back_step(n):
         for d in (1, 7, 2, 6, 3, 5, 4):
@@ -469,6 +479,7 @@
 
     a2 = near(sum_y, 0, p.ys, p.at_y, a1, ya1, ya2)
     b2 = near(sum_x, 4, p.xs, p.at_x, b1, xb1, xb2)
+    back_start(1)
     back_step(0)
     back_send(0)
     back_step(1)
@@ -480,15 +491,28 @@
     b4 = near(narrow_y, 4, p.ys, p.at_y, b3, yb1, yb2)
     close(narrow_x, 0, p.xs, a4, xa2)
     close(narrow_y, 4, p.ys, b4, yb2)
-    zsum = [cp.start(part.at[p.zs(d), x, sub(y), :], zbuf.at[d], p.at_z(d)) for d in order]
+    zsum = [
+        [
+            cp.start(
+                part.at[p.zs(d), x, rows_of(piece), :],
+                zbuf.at[d, pl.ds(*piece), :],
+                p.at_z(d),
+            )
+            for d in order
+        ]
+        for piece in pieces
+    ]
     back_send(1)
-    for copy in zsum:
-        copy.wait_recv()
-    total = part[z, x, sub(y), :].astype(F32)
-    for d in range(1, NZ):
-        total = total + zbuf[d].astype(F32)
-    fin[x, y] = total.astype(BF16)
-    last = [cp.start(fin.at[x, y], fin.at[x, y], p.at_dp(d)) for d in range(1, NX * NX)]
+    last = []
+    for piece, arriving in zip(pieces, zsum):
+        for copy in arriving:
+            copy.wait_recv()
+        total = part[z, x, rows_of(piece), :].astype(F32)
+        for d in range(1, NZ):
+            total = total + zbuf[d, pl.ds(*piece), :].astype(F32)
+        fin[x, y, pl.ds(*piece), :] = total.astype(BF16)
+        block = fin.at[x, y, pl.ds(*piece), :]
+        last += [cp.start(block, block, p.at_dp(d)) for d in range(1, NX * NX)]
     for copy in last:
         copy.wait_recv()
     written = local(fin, fin_ref, 15)
@@ -523,10 +547,10 @@
         out_specs=(anyspace,) * 4,
         scratch_shapes=[
             pltpu.SMEM((NZ * CAP,), jnp.int32),
-            scratch(SLOTS, PIECE, 512),
-            scratch(SLOTS, PIECE, DE - 512),
-            scratch(NZ, 2, PIECE, 512),
-            scratch(NZ, 2, PIECE, DE - 512),
+            scratch(SLOTS, PIECE, SPLIT),
+            scratch(SLOTS, PIECE, DE - SPLIT),
+            scratch(NZ, 2, PIECE, SPLIT),
+            scratch(NZ, 2, PIECE, DE - SPLIT),
             scratch(2, NLEN, DE),
             scratch(NZ, 2, 4, WROWS, HD),
             scratch(DE, FFE),
@@ -545,10 +569,10 @@
             scratch(NZ, ROWS, 2 * HD),
             scratch(NZ, 4, WROWS, HD),
             scratch(2, NLEN, DE),
-            scratch(1 + SLOTS // 2, PIECE, 512),
-            scratch(1 + SLOTS // 2, PIECE, DE - 512),
-            scratch(NZ, CAP, PIECE, 512),
-            scratch(NZ, CAP, PIECE, DE - 512),
+            scratch(1 + SLOTS // 2, PIECE, SPLIT),
+            scratch(1 + SLOTS // 2, PIECE, DE - SPLIT),
+            scratch(NZ, CAP, PIECE, SPLIT),
+            scratch(NZ, CAP, PIECE, DE - SPLIT),
             scratch(2, 2, 4, WSUB, HD),
             scratch(2, 4, 4, WSUB, HD),
             scratch(2, 2, WSUB, HD),

time: 115 us -> 113 us (0.983)
  Pallas kernels: 114 us -> 112 us
    pallas_call x1, Pallas kernels: 111 us -> 109 us  [whole(): pl.pallas_call(whole_kernel, out_shape=(jax.ShapeDtypeStruct((TOKENS, wid...]
where the time goes in v5:
time: 113 us
  Pallas kernels  112 us (99%)
    pallas_call x1, Pallas kernels, whole(): pl.pallas_call(whole_kernel, out_shape=(jax.ShapeDtypeStruct((TOKENS, wid...  109 us
    pallas_call x1, Pallas kernels, place(): pl.pallas_call(place_kernel, out_shape=(*shapes, grad, grad), in_specs=[a...  2.9 us

profile of v5, /device:TPU:1, one launch (start us, length us, event | category | flops | bytes accessed | tf_op | source)
XLA Modules:
  0.0 113.1 jit_solution(1573335349726354253)
XLA Ops:
  0.6 109.4 %whole.1 = (bf16[128,2048]{1,0:T(8,128)(2,1)}, bf16[128,2048]{1,0:T(8,128)(2,1)}, bf16[4,128,896]{2,1,0:T(8,128)(2,1)}, bf16[4,4,112,128]{3,2,1,0:T(8,128)(2,1)}) custom-call(s32[32]{0:T(128)} %bitcast.14, f32[896]{0:T(1024)} %gain_ref.1, bf16[4,128,896]{2,1,0:T(8,128)(2,1)} %bitcast.9, bf16[2,448,128]{2,1,0:T(8,128)(2,1)} %bitcast.12, ...), custom_call_target="tpu_custom_call" | custom-call | tf_op jit(solution)/shard_map/whole/pallas_call | solution.py:538
  110.0 2.9 %place.1 = (bf16[128,2048]{1,0:T(8,128)(2,1)}, bf16[128,2048]{1,0:T(8,128)(2,1)}, bf16[4,128,896]{2,1,0:T(8,128)(2,1)}, f32[896,128]{1,0:T(8,128)}, f32[896,128]{1,0:T(8,128)}) custom-call(bf16[128,2048]{1,0:T(8,128)(2,1)} %get-tuple-element.14.att, bf16[128,2048]{1,0:T(8,128)(2,1)} %get-tuple-element.15.qg, bf16[4,128,896]{2,1,0:T(8,128)(2,1)} %get-tuple-element.16.pg, ...), custom_call_target="tpu_custom_call" | custom-call | tf_op jit(solution)/shard_map/place/pallas_call | solution.py:635

commit v6 on v5

--- a/solution.py
+++ b/solution.py
@@ -104,7 +104,7 @@
 
 
 COPIES = 192
-SPLIT = 640
+SPLIT = 512
 HALVES = (slice(0, SPLIT), slice(SPLIT, DE))
 GROUP = 8
 TILE = 256

time: 113 us -> 110 us (0.973)
  Pallas kernels: 112 us -> 109 us
    pallas_call x1, Pallas kernels: 109 us -> 106 us  [whole(): pl.pallas_call(whole_kernel, out_shape=(jax.ShapeDtypeStruct((TOKENS, wid...]
where the time goes in v6:
time: 110 us
  Pallas kernels  109 us (99%)
    pallas_call x1, Pallas kernels, whole(): pl.pallas_call(whole_kernel, out_shape=(jax.ShapeDtypeStruct((TOKENS, wid...  106 us
    pallas_call x1, Pallas kernels, place(): pl.pallas_call(place_kernel, out_shape=(*shapes, grad, grad), in_specs=[a...  2.9 us

profile of v6, /device:TPU:1, one launch (start us, length us, event | category | flops | bytes accessed | tf_op | source)
XLA Modules:
  0.0 110.2 jit_solution(6762075921647680992)
XLA Ops:
  0.6 106.5 %whole.1 = (bf16[128,2048]{1,0:T(8,128)(2,1)}, bf16[128,2048]{1,0:T(8,128)(2,1)}, bf16[4,128,896]{2,1,0:T(8,128)(2,1)}, bf16[4,4,112,128]{3,2,1,0:T(8,128)(2,1)}) custom-call(s32[32]{0:T(128)} %bitcast.14, f32[896]{0:T(1024)} %gain_ref.1, bf16[4,128,896]{2,1,0:T(8,128)(2,1)} %bitcast.9, bf16[2,448,128]{2,1,0:T(8,128)(2,1)} %bitcast.12, ...), custom_call_target="tpu_custom_call" | custom-call | tf_op jit(solution)/shard_map/whole/pallas_call | solution.py:538
  107.1 2.9 %place.1 = (bf16[128,2048]{1,0:T(8,128)(2,1)}, bf16[128,2048]{1,0:T(8,128)(2,1)}, bf16[4,128,896]{2,1,0:T(8,128)(2,1)}, f32[896,128]{1,0:T(8,128)}, f32[896,128]{1,0:T(8,128)}) custom-call(bf16[128,2048]{1,0:T(8,128)(2,1)} %get-tuple-element.14.att, bf16[128,2048]{1,0:T(8,128)(2,1)} %get-tuple-element.15.qg, bf16[4,128,896]{2,1,0:T(8,128)(2,1)} %get-tuple-element.16.pg, ...), custom_call_target="tpu_custom_call" | custom-call | tf_op jit(solution)/shard_map/place/pallas_call | solution.py:635
